TPU v7x, 128 devices: a whole 4x4x4 slice. The times are simulated.
128 devices in a mesh: gx: 8 (over z, core), gy: 16 (over y, x).
Axes of the slice: x: 4, y: 4, z: 4, core: 2. Of those that a mesh axis runs over, the one named last changes fastest.
Arguments:
- cotangent: float32 [6, 256, 256, 128], P(None, 'gx', 'gy'), may hold values from -3000 to 3000
- diffusion: float32 [256, 256, 128], P('gx', 'gy'), may hold values from 50 to 2000
- phase: int32 [256, 256, 128], P('gx', 'gy'), may hold values 0 or 1
- courant: float32 [3, 256, 256, 128], P(None, 'gx', 'gy'), may hold values from 0.02 to 0.3
- upwind: int32 [3, 256, 256, 128], P(None, 'gx', 'gy'), may hold values 0 or 1
Outputs:
- grad: float32 [6, 256, 256, 128], P(None, 'gx', 'gy')
All inputs are finite; a program needn't handle non-finite values. No bound on the sum of `phase` or of `upwind` on one device may be relied on, other than what follows from the above.
Results may differ from a plain program's by a relative error of at most 0.00019.
Values sent between devices are 32-bit elements; how exact they have to be, the bound alone decides.
A program may use at most 128 MiB of HBM per device.

v0:
```python
import functools

import jax
import jax.numpy as jnp
from jax import lax
from jax.experimental import pallas as pl
from jax.experimental.pallas import tpu as pltpu
from jax.sharding import PartitionSpec as P

MESH = pl.DeviceIdType.MESH
C, X, Y, Z = 6, 32, 16, 128
NI, NJ = 8, 16
LINES = X * Y
PAD = 24
PLANES = X + 2
PITCH = PLANES * PAD + 8
HALF = C * 2
PACK = 2 * HALF
f32 = jnp.float32


def split(values):
    high = values.astype(jnp.bfloat16)
    low = (values - high.astype(f32)).astype(jnp.bfloat16)
    return jnp.concatenate([high, low], axis=1)


def body(
    cot_h, dif_h, pha_h, cou_h, upw_h, out_h,
    cot, dif, pha, cou, upw, ec,
    zt, zw, zo, zb, tri,
    yb, ya, yw, yo, yr, yf, ay, ayh,
    xe, xb, xa, xw, xo, xr,
    csy, csx, rcy, rcx, ky, kx, gl,
    sty, tty, oty, rty, stx, ttx, otx, rtx, ext,
    fsy, fry, fsx, frx,
    c0, ax, bx, ayp, byp, azn, bzp, fb,
    in_sem, out_sem,
    s_cy, r_cy, s_cx, r_cx, s_fy, r_fy, s_fx, r_fx,
    s_ty, r_ty, s_oy, r_oy, s_tx, r_tx, s_ox, r_ox, s_ex, r_ex,
):
    i = lax.axis_index("gx")
    j = lax.axis_index("gy")
    inext, iprev = lax.rem(i + 1, NI), lax.rem(i + NI - 1, NI)
    jnext, jprev = lax.rem(j + 1, NJ), lax.rem(j + NJ - 1, NJ)

    loads = [
        pltpu.make_async_copy(dif_h, dif, in_sem.at[0]),
        pltpu.make_async_copy(pha_h, pha, in_sem.at[1]),
        pltpu.make_async_copy(cot_h, cot, in_sem.at[2]),
        pltpu.make_async_copy(cou_h, cou, in_sem.at[3]),
        pltpu.make_async_copy(upw_h, upw, in_sem.at[4]),
    ]
    for load in loads:
        load.start()

    barrier = pltpu.get_barrier_semaphore()

    def greet_y(d, _):
        pl.semaphore_signal(barrier, inc=1, device_id=(i, lax.rem(j + d, NJ)), device_id_type=MESH)
        return 0

    def greet_x(d, _):
        pl.semaphore_signal(barrier, inc=1, device_id=(lax.rem(i + d, NI), j), device_id_type=MESH)
        return 0

    lax.fori_loop(1, NJ, greet_y, 0)
    lax.fori_loop(1, NI, greet_x, 0)

    @pl.when(i != 0)
    def _():
        pl.semaphore_signal(barrier, inc=1, device_id=(0, jnext), device_id_type=MESH)

    @pl.when(i != NI - 1)
    def _():
        pl.semaphore_signal(barrier, inc=1, device_id=(NI - 1, jprev), device_id_type=MESH)

    loads[0].wait()
    loads[1].wait()
    ec[...] = 1.0 / (dif[...] * (1.0 + 3.0 * pha[...].astype(f32)))

    for q in range(X // 8):
        xs = pl.ds(q * 8, 8)
        cells = [ec[pl.ds(q * 8 * Y + y, 8, stride=Y), :] for y in range(Y)]
        theta = jnp.ones((8, Z), f32)
        delta = jnp.ones((8, Z), f32)
        for y in range(Y):
            yb[y, xs, :] = theta
            delta = delta + cells[y] * theta
            theta = theta + delta
        rn = 1.0 / theta
        yr[xs, :] = rn
        phi = jnp.ones((8, Z), f32)
        delta = jnp.ones((8, Z), f32)
        after = jnp.ones((8, Z), f32)
        at = (q % 2) * 8 * 8 + q // 2
        for y in range(Y - 1, -1, -1):
            a = phi * rn
            b = yb[y, xs, :] * rn
            ya[y, xs, :] = a
            yb[y, xs, :] = b
            yw[y, xs, :] = 1.0 / (b * after)
            yo[y, xs, :] = b * cells[y]
            if y == Y - 1:
                csy[pl.ds(at + 4, 8, stride=8), :] = b
            if y == 0:
                csy[pl.ds(at, 8, stride=8), :] = a
            after = b
            delta = delta + cells[y] * phi
            phi = phi + delta
        csy[pl.ds(at + 2, 8, stride=8), :] = rn

    def x_factor(lo):
        rows = pl.ds(lo, 16)
        one = jnp.ones((16, Z), f32)

        def up(x, carry):
            theta, delta = carry
            xb[x, rows, :] = theta
            delta = delta + xe[x, rows, :] * theta
            return theta + delta, delta

        theta, _ = lax.fori_loop(0, X, up, (one, one), unroll=8)
        rn = 1.0 / theta
        xr[rows, :] = rn

        def down(step, carry):
            x = X - 1 - step
            phi, delta, after, _ = carry
            cell = xe[x, rows, :]
            a = phi * rn
            b = xb[x, rows, :] * rn
            xa[x, rows, :] = a
            xb[x, rows, :] = b
            xw[x, rows, :] = 1.0 / (b * after)
            xo[x, rows, :] = b * cell
            delta = delta + cell * phi
            return phi + delta, delta, b, a

        _, _, _, first = lax.fori_loop(0, X, down, (one, one, one, one), unroll=8)
        return first, rn

    for x in range(X):
        xe[x, 0:Y, :] = ec[x * Y : (x + 1) * Y, :]
    first, rn = x_factor(0)
    last = xb[X - 1, 0:Y, :]
    for r in range(2):
        csx[pl.ds(r, 8, stride=8), :] = first[r * 8 : r * 8 + 8]
        csx[pl.ds(2 + r, 8, stride=8), :] = rn[r * 8 : r * 8 + 8]
        csx[pl.ds(4 + r, 8, stride=8), :] = last[r * 8 : r * 8 + 8]

    loads[3].wait()
    loads[4].wait()
    fsy[0, 0] = ec[pl.ds(0, X, stride=Y), :]
    fsy[1, 0] = ec[pl.ds(Y - 1, X, stride=Y), :]
    fsy[0, 1] = upw[1, pl.ds(0, X, stride=Y), :].astype(f32) * cou[1, pl.ds(0, X, stride=Y), :]
    fsy[1, 1] = (1.0 - upw[1, pl.ds(Y - 1, X, stride=Y), :].astype(f32)) * cou[1, pl.ds(Y - 1, X, stride=Y), :]
    fsx[0] = upw[0, 0:Y, :].astype(f32) * cou[0, 0:Y, :] * ec[0:Y, :]
    fsx[1] = (1.0 - upw[0, LINES - Y : LINES, :].astype(f32)) * cou[0, LINES - Y : LINES, :] * ec[LINES - Y : LINES, :]

    outer = (i == 0) | (i == NI - 1)
    pl.semaphore_wait(barrier, NI + NJ - 2 + jnp.where(outer, NI - 1, 0))

    def exchange(src, dst, send, recv, rows, k, axis):
        here = j if axis == "gy" else i
        return pltpu.make_async_remote_copy(
            src_ref=src.at[pl.ds(pl.multiple_of(k * rows, 8), rows), :],
            dst_ref=dst.at[pl.ds(pl.multiple_of(here * rows, 8), rows), :],
            send_sem=send.at[k],
            recv_sem=recv.at[here],
            device_id={axis: k},
            device_id_type=MESH,
        )

    def arrival(src, dst, send, recv, rows, k, axis):
        return pltpu.make_async_remote_copy(
            src_ref=src.at[pl.ds(pl.multiple_of(k * rows, 8), rows), :],
            dst_ref=dst.at[pl.ds(pl.multiple_of(k * rows, 8), rows), :],
            send_sem=send.at[k],
            recv_sem=recv.at[k],
            device_id={axis: k},
            device_id_type=MESH,
        )

    def count_of(axis):
        return NJ if axis == "gy" else NI

    def send_all(src, dst, send, recv, rows, axis):
        n = count_of(axis)
        here = j if axis == "gy" else i
        mine = pl.ds(pl.multiple_of(here * rows, 8), rows)

        def step(d, _):
            exchange(src, dst, send, recv, rows, lax.rem(here + d, n), axis).start()
            return 0

        lax.fori_loop(1, n, step, 0)
        dst[mine, :] = src[mine, :]

    def recv_all(src, dst, send, recv, rows, axis):
        n = count_of(axis)
        here = j if axis == "gy" else i

        def step(d, _):
            arrival(src, dst, send, recv, rows, lax.rem(here + d, n), axis).wait_recv()
            return 0

        lax.fori_loop(1, n, step, 0)

    def sent_all(src, dst, send, recv, rows, axis):
        n = count_of(axis)
        here = j if axis == "gy" else i

        def step(d, _):
            arrival(src, dst, send, recv, rows, lax.rem(here + d, n), axis).wait_send()
            return 0

        lax.fori_loop(1, n, step, 0)

    coup_y = (csy, rcy, s_cy, r_cy, 8, "gy")
    coup_x = (csx, rcx, s_cx, r_cx, 8, "gx")
    tot_y = (sty, tty, s_ty, r_ty, PACK, "gy")
    ret_y = (oty, rty, s_oy, r_oy, PACK, "gy")
    tot_x = (stx, ttx, s_tx, r_tx, PACK, "gx")
    ret_x = (otx, rtx, s_ox, r_ox, PACK, "gx")

    def face(src, dst, send, recv, slot, axis, to):
        return pltpu.make_async_remote_copy(
            src_ref=src.at[slot], dst_ref=dst.at[slot], send_sem=send.at[slot], recv_sem=recv.at[slot],
            device_id={axis: to}, device_id_type=MESH,
        )

    faces = [
        face(fsy, fry, s_fy, r_fy, 0, "gy", jprev),
        face(fsy, fry, s_fy, r_fy, 1, "gy", jnext),
        face(fsx, frx, s_fx, r_fx, 0, "gx", iprev),
        face(fsx, frx, s_fx, r_fx, 1, "gx", inext),
    ]
    send_all(*coup_y)
    send_all(*coup_x)
    for f in faces:
        f.start()

    lane = lax.broadcasted_iota(jnp.int32, (64, Z), 1)

    def z_factor(block, _):
        rows = pl.ds(pl.multiple_of(block * 64, 64), 64)
        e = ec[rows, :]
        p11, p12, p21, p22 = 1.0 + e, jnp.ones_like(e), e, jnp.ones_like(e)
        step = 1
        while step < Z:
            keep = lane < step
            q11 = jnp.where(keep, 1.0, pltpu.roll(p11, step, 1))
            q12 = jnp.where(keep, 0.0, pltpu.roll(p12, step, 1))
            q21 = jnp.where(keep, 0.0, pltpu.roll(p21, step, 1))
            q22 = jnp.where(keep, 1.0, pltpu.roll(p22, step, 1))
            p11, p12, p21, p22 = (
                p11 * q11 + p12 * q21,
                p11 * q12 + p12 * q22,
                p21 * q11 + p22 * q21,
                p21 * q12 + p22 * q22,
            )
            step *= 2
        theta = p11 + p12
        before = jnp.where(lane < 1, 1.0, pltpu.roll(theta, 1, 1))
        zt[rows, :] = before
        zw[rows, :] = 1.0 / (theta * before)
        zo[rows, :] = before * e
        return 0

    lax.fori_loop(0, LINES // 64, z_factor, 0)

    row = lax.rem(lax.broadcasted_iota(jnp.int32, (2 * Z, Z), 0), Z)
    col = lax.broadcasted_iota(jnp.int32, (2 * Z, Z), 1)
    tri[0] = (row <= col).astype(f32).astype(jnp.bfloat16)
    tri[1] = (row >= col).astype(f32).astype(jnp.bfloat16)

    loads[2].wait()

    def z_and_y(q):
        rows = pl.ds(q * 8 * Y, 8 * Y)
        scale, weight, finish = zt[rows, :], zw[rows, :], zo[rows, :]
        sums = [
            jnp.dot(split(cot[c, rows, :] * scale), tri[0], preferred_element_type=f32) for c in range(C)
        ]
        for c in range(C):
            whole = jnp.dot(split(sums[c] * weight), tri[1], preferred_element_type=f32)
            zb[c, rows, :] = whole * finish
        xs = pl.ds(q * 8, 8)
        heads = [jnp.zeros((8, Z), f32) for _ in range(C)]
        tails = [jnp.zeros((8, Z), f32) for _ in range(C)]
        for y in range(Y):
            a, b = ya[y, xs, :], yb[y, xs, :]
            for c in range(C):
                value = zb[c, pl.ds(q * 8 * Y + y, 8, stride=Y), :]
                heads[c] = heads[c] + a * value
                tails[c] = tails[c] + b * value
                yf[c, y, xs, :] = tails[c]
        at = (q % 2) * 8 * PACK + (q // 2) * C
        for c in range(C):
            sty[pl.ds(at + c, 8, stride=PACK), :] = heads[c]
            sty[pl.ds(at + HALF + c, 8, stride=PACK), :] = tails[c]

    def wave(w):
        def step(d, _):
            k = lax.rem(j + d, 8) + 8 * w

            @pl.when(k != j)
            def _():
                exchange(*tot_y[:5], k, "gy").start()

            return 0

        lax.fori_loop(0, 8, step, 0)

    z_and_y(0)
    z_and_y(2)
    wave(0)
    z_and_y(1)
    z_and_y(3)
    wave(1)
    mine_y = pl.ds(pl.multiple_of(j * PACK, 8), PACK)
    tty[mine_y, :] = sty[mine_y, :]

    def reduce_factor(count, couplings, factors):
        def pair(base, t):
            return jnp.concatenate(
                [
                    jnp.broadcast_to(couplings[pl.ds(base + 2 * t, 1), :], (C, Z)),
                    jnp.broadcast_to(couplings[pl.ds(base + 2 * t + 1, 1), :], (C, Z)),
                ],
                axis=0,
            )

        edge = jnp.zeros((HALF, Z), f32)
        for m in range(count):
            a1, b1, bn = pair(m * 8, 0), pair(m * 8, 1), pair(m * 8, 2)
            alpha = 1.0 / (1.0 - a1 * edge)
            alpha_a = a1 * alpha
            forward = b1 * alpha
            back = b1 * edge
            factors[0, m, 0:HALF, :] = alpha
            factors[1, m, 0:HALF, :] = alpha_a
            factors[2, m, 0:HALF, :] = forward
            factors[3, m, 0:HALF, :] = edge
            factors[4, m, 0:HALF, :] = back * alpha
            factors[5, m, 0:HALF, :] = b1 + back * alpha_a
            edge = bn + back * forward

    def reduce_solve(count, totals, factors, results):
        gain = jnp.zeros((HALF, Z), f32)
        for m in range(count):
            head = totals[m * PACK : m * PACK + HALF, :]
            tail = totals[m * PACK + HALF : m * PACK + PACK, :]
            gl[0, m, 0:HALF, :] = gain
            gl[1, m, 0:HALF, :] = factors[0, m, 0:HALF, :] * head + factors[1, m, 0:HALF, :] * gain
            gain = tail + factors[4, m, 0:HALF, :] * head + factors[5, m, 0:HALF, :] * gain
        later = jnp.zeros((HALF, Z), f32)
        for m in range(count - 1, -1, -1):
            results[m * PACK + HALF : m * PACK + PACK, :] = later
            later = gl[1, m, 0:HALF, :] + factors[2, m, 0:HALF, :] * later
            results[m * PACK : m * PACK + HALF, :] = gl[0, m, 0:HALF, :] + factors[3, m, 0:HALF, :] * later

    recv_all(*coup_y)
    reduce_factor(NJ, rcy, ky)

    recv_all(*tot_y)
    reduce_solve(NJ, tty, ky, oty)
    send_all(*ret_y)

    recv_all(*coup_x)
    reduce_factor(NI, rcx, kx)
    for f in faces:
        f.wait_recv()

    for x in range(X):
        xe[x, 16:24, :] = jnp.broadcast_to(fry[1, 0, x : x + 1, :], (8, Z))
        xe[x, 24:32, :] = jnp.broadcast_to(fry[0, 0, x : x + 1, :], (8, Z))
    x_factor(16)

    low_ok = jnp.where(j > 0, 1.0, 0.0).astype(f32)
    high_ok = jnp.where(j < NJ - 1, 1.0, 0.0).astype(f32)
    lane16 = lax.broadcasted_iota(jnp.int32, (Y, Z), 1)

    def coefficients(x, _):
        rows = pl.ds(pl.multiple_of(x * Y, Y), Y)
        shifted = pl.ds(pl.multiple_of(x * Y + Y, Y), Y)
        padded = pl.ds(pl.multiple_of(x * PAD + 8, 8), Y)
        flux = [cou[d, rows, :] for d in range(3)]
        ahead = [upw[d, rows, :].astype(f32) * flux[d] for d in range(3)]
        behind = [flux[d] - ahead[d] for d in range(3)]
        c0[rows, :] = 1.0 + (behind[0] - ahead[0]) + (behind[1] - ahead[1]) + (behind[2] - ahead[2])
        ax[shifted, :] = ahead[0]
        bx[shifted, :] = behind[0]
        ayp[padded, :] = ahead[1]
        byp[padded, :] = behind[1]
        azn[rows, :] = jnp.where(lane16 < Z - 1, pltpu.roll(ahead[2], Z - 1, 1), 0.0)
        bzp[rows, :] = jnp.where(lane16 > 0, pltpu.roll(behind[2], 1, 1), 0.0)
        return 0

    lax.fori_loop(0, X, coefficients, 0, unroll=2)
    bx[0:Y, :] = frx[1]
    ax[(X + 1) * Y : (X + 2) * Y, :] = frx[0]
    byp[pl.ds(7, X, stride=PAD), :] = fry[1, 1] * low_ok
    ayp[pl.ds(PAD, X, stride=PAD), :] = fry[0, 1] * high_ok
    ayh[...] = jnp.zeros_like(ayh)

    recv_all(*ret_y)

    for q in (0, 2, 1, 3):
        xs = pl.ds(q * 8, 8)
        at = (q % 2) * 8 * PACK + (q // 2) * C
        below, above, live = [], [], []
        for c in range(C):
            left = rty[pl.ds(at + c, 8, stride=PACK), :]
            right = rty[pl.ds(at + HALF + c, 8, stride=PACK), :]
            ayh[pl.ds(q * 8 * 16 + c, 8, stride=16), :] = left * fry[1, 0, xs, :]
            ayh[pl.ds(q * 8 * 16 + 8 + c, 8, stride=16), :] = right * fry[0, 0, xs, :]
            below.append(left * yr[xs, :])
            live.append(right)
        for y in range(Y - 1, -1, -1):
            weight, finish = yw[y, xs, :], yo[y, xs, :]
            for c in range(C):
                live[c] = live[c] + weight * (yf[c, y, xs, :] + below[c])
                ay[c, pl.ds(q * 8 * Y + y, 8, stride=Y), :] = live[c] * finish

    def x_totals(x, carry):
        heads, tails, halo = carry
        rows = pl.ds(pl.multiple_of(x * Y, Y), Y)
        a, b = xa[x, 0:Y, :], xb[x, 0:Y, :]
        new_heads, new_tails = [], []
        for c in range(C):
            value = ay[c, rows, :]
            new_heads.append(heads[c] + a * value)
            tail = tails[c] + b * value
            new_tails.append(tail)
            ay[c, rows, :] = tail
        halo = halo + xb[x, 16:32, :] * ayh[rows, :]
        ayh[rows, :] = halo
        return tuple(new_heads), tuple(new_tails), halo

    none = jnp.zeros((Y, Z), f32)
    heads, tails, _ = lax.fori_loop(0, X, x_totals, ((none,) * C, (none,) * C, none), unroll=2)
    for c in range(C):
        for r in range(2):
            stx[pl.ds(r * C + c, 8, stride=PACK), :] = heads[c][r * 8 : r * 8 + 8]
            stx[pl.ds(HALF + r * C + c, 8, stride=PACK), :] = tails[c][r * 8 : r * 8 + 8]
    send_all(*tot_x)
    sent_all(*coup_y)
    sent_all(*coup_x)
    sent_all(*tot_y)
    sent_all(*ret_y)
    for f in faces:
        f.wait_send()
    recv_all(*tot_x)
    reduce_solve(NI, ttx, kx, otx)
    send_all(*ret_x)

    def extra(m, slot, to):
        return pltpu.make_async_remote_copy(
            src_ref=otx.at[pl.ds(pl.multiple_of(m * PACK, 8), PACK), :],
            dst_ref=ext.at[slot, pl.ds(0, PACK), :],
            send_sem=s_ex.at[slot, m],
            recv_sem=r_ex.at[slot],
            device_id=(m, to),
            device_id_type=MESH,
        )

    @pl.when(i == 0)
    def _():
        for m in range(NI):
            extra(m, 1, jprev).start()

    @pl.when(i == NI - 1)
    def _():
        for m in range(NI):
            extra(m, 0, jnext).start()

    recv_all(*ret_x)
    extra(0, 0, jnext).wait_recv()
    extra(0, 1, jprev).wait_recv()

    lefts, rights = [], []
    for c in range(C):
        left = jnp.concatenate([rtx[pl.ds(r * C + c, 8, stride=PACK), :] for r in range(2)], axis=0)
        right = jnp.concatenate([rtx[pl.ds(HALF + r * C + c, 8, stride=PACK), :] for r in range(2)], axis=0)
        fb[pl.ds(c * PITCH + 8, Y), :] = left
        fb[pl.ds(c * PITCH + (X + 1) * PAD + 8, Y), :] = right
        lefts.append(left * xr[0:Y, :])
        rights.append(right)
    left_halo = jnp.concatenate([ext[0, 6:14, :], ext[1, 0:8, :]], axis=0) * xr[16:32, :]
    right_halo = jnp.concatenate([ext[0, 18:26, :], ext[1, 12:20, :]], axis=0)

    def x_finish(step, carry):
        x = X - 1 - step
        live, halo = carry
        rows = pl.ds(pl.multiple_of(x * Y, Y), Y)
        weight, finish = xw[x, 0:Y, :], xo[x, 0:Y, :]
        out = []
        for c in range(C):
            value = live[c] + weight * (ay[c, rows, :] + lefts[c])
            fb[pl.ds(pl.multiple_of(c * PITCH + (x + 1) * PAD + 8, 8), Y), :] = value * finish
            out.append(value)
        halo = halo + xw[x, 16:32, :] * (ayh[rows, :] + left_halo)
        edge = halo * xo[x, 16:32, :]
        fb[pl.ds((x + 1) * PAD + 7, 8, stride=PITCH), :] = edge[0:8]
        fb[pl.ds((x + 2) * PAD, 8, stride=PITCH), :] = edge[8:16]
        return tuple(out), halo

    lax.fori_loop(0, X, x_finish, (tuple(rights), right_halo), unroll=2)

    def advect(x, _):
        rows = pl.ds(pl.multiple_of(x * Y, Y), Y)
        middle = c0[rows, :]
        from_x, to_x = bx[rows, :], ax[pl.ds(pl.multiple_of((x + 2) * Y, Y), Y), :]
        from_y, to_y = byp[pl.ds(x * PAD + 7, Y), :], ayp[pl.ds(x * PAD + 9, Y), :]
        from_z, to_z = bzp[rows, :], azn[rows, :]
        for c in range(C):
            at = c * PITCH + (x + 1) * PAD + 8
            value = fb[pl.ds(pl.multiple_of(at, 8), Y), :]
            result = middle * value
            result += to_x * fb[pl.ds(pl.multiple_of(at + PAD, 8), Y), :]
            result -= from_x * fb[pl.ds(pl.multiple_of(at - PAD, 8), Y), :]
            result += to_y * fb[pl.ds(at + 1, Y), :]
            result -= from_y * fb[pl.ds(at - 1, Y), :]
            result += to_z * pltpu.roll(value, Z - 1, 1)
            result -= from_z * pltpu.roll(value, 1, 1)
            cot[c, rows, :] = result
        return 0

    stores = []
    for part in range(4):
        lax.fori_loop(part * 8, part * 8 + 8, advect, 0, unroll=2)
        rows = pl.ds(part * 8 * Y, 8 * Y)
        store = pltpu.make_async_copy(cot.at[:, rows, :], out_h.at[:, rows, :], out_sem.at[part])
        store.start()
        stores.append(store)

    sent_all(*tot_x)
    sent_all(*ret_x)

    @pl.when(i == 0)
    def _():
        for m in range(NI):
            extra(m, 1, jprev).wait_send()

    @pl.when(i == NI - 1)
    def _():
        for m in range(NI):
            extra(m, 0, jnext).wait_send()

    for store in stores:
        store.wait()


def on_device(cotangent, diffusion, phase, courant, upwind):
    def vm(*shape, dtype=f32):
        return pltpu.VMEM(shape, dtype)

    dma = pltpu.SemaphoreType.DMA
    scratch = [
        vm(C, LINES, Z), vm(LINES, Z), vm(LINES, Z, dtype=jnp.int32), vm(3, LINES, Z), vm(3, LINES, Z, dtype=jnp.int32),
        vm(LINES, Z),
        vm(LINES, Z), vm(LINES, Z), vm(LINES, Z), vm(C, LINES, Z), vm(2, 2 * Z, Z, dtype=jnp.bfloat16),
        vm(Y, X, Z), vm(Y, X, Z), vm(Y, X, Z), vm(Y, X, Z), vm(X, Z), vm(C, Y, X, Z), vm(C, LINES, Z), vm(X * 16, Z),
        vm(X, 32, Z), vm(X, 32, Z), vm(X, 32, Z), vm(X, 32, Z), vm(X, 32, Z), vm(32, Z),
        vm(NJ * 8, Z), vm(NI * 8, Z), vm(NJ * 8, Z), vm(NI * 8, Z), vm(6, NJ, 16, Z), vm(6, NI, 16, Z), vm(2, NJ, 16, Z),
        vm(NJ * PACK, Z), vm(NJ * PACK, Z), vm(NJ * PACK, Z), vm(NJ * PACK, Z),
        vm(NI * PACK, Z), vm(NI * PACK, Z), vm(NI * PACK, Z), vm(NI * PACK, Z), vm(2, 32, Z),
        vm(2, 2, X, Z), vm(2, 2, X, Z), vm(2, Y, Z), vm(2, Y, Z),
        vm(LINES, Z), vm(LINES + 2 * Y, Z), vm(LINES + 2 * Y, Z), vm(X * PAD + 8, Z), vm(X * PAD + 8, Z), vm(LINES, Z), vm(LINES, Z),
        vm(8 * PITCH, Z),
        dma((5,)), dma((4,)),
        dma((NJ,)), dma((NJ,)), dma((NI,)), dma((NI,)), dma((2,)), dma((2,)), dma((2,)), dma((2,)),
        dma((NJ,)), dma((NJ,)), dma((NJ,)), dma((NJ,)), dma((NI,)), dma((NI,)), dma((NI,)), dma((NI,)),
        dma((2, NI)), dma((2,)),
    ]
    out = pl.pallas_call(
        body,
        out_shape=jax.ShapeDtypeStruct((C, LINES, Z), f32),
        in_specs=[pl.BlockSpec(memory_space=pl.ANY)] * 5,
        out_specs=pl.BlockSpec(memory_space=pl.ANY),
        scratch_shapes=scratch,
        compiler_params=pltpu.CompilerParams(
            collective_id=0, has_side_effects=True, vmem_limit_bytes=48 * 1024 * 1024
        ),
    )(
        cotangent.reshape(C, LINES, Z),
        diffusion.reshape(LINES, Z),
        phase.reshape(LINES, Z),
        courant.reshape(3, LINES, Z),
        upwind.reshape(3, LINES, Z),
    )
    return out.reshape(C, X, Y, Z)


def solution(mesh):
    placed = (
        P(None, "gx", "gy", None),
        P("gx", "gy", None),
        P("gx", "gy", None),
        P(None, "gx", "gy", None),
        P(None, "gx", "gy", None),
    )
    return jax.shard_map(
        on_device, mesh=mesh, in_specs=placed, out_specs=P(None, "gx", "gy", None), check_vma=False
    )
```

profile of v0, /device:TPU:1, one launch (start us, length us, event | category | flops | bytes accessed | tf_op | source)
XLA Modules:
  0.0 48.4 jit_solution(13744800385214141927)
XLA Ops:
  0.0 0.0 copy-start
  0.0 1.4 %copy-done = f32[6,32,16,128]{3,2,1,0:T(8,128)S(1)} copy-done((f32[6,32,16,128]{3,2,1,0:T(8,128)S(1)}, f32[6,32,16,128]{3,2,1,0:T(8,128)}, u32[]{:S(2)}) %copy-start) | copy-done | bytes 1572888
  1.4 0.0 copy-start.1
  1.4 1.1 %copy-done.1 = f32[3,32,16,128]{3,2,1,0:T(8,128)S(1)} copy-done((f32[3,32,16,128]{3,2,1,0:T(8,128)S(1)}, f32[3,32,16,128]{3,2,1,0:T(8,128)}, u32[]{:S(2)}) %copy-start.1) | copy-done | bytes 786456
  2.5 0.0 copy-start.2
  2.5 1.1 %copy-done.2 = s32[3,32,16,128]{3,2,1,0:T(8,128)S(1)} copy-done((s32[3,32,16,128]{3,2,1,0:T(8,128)S(1)}, s32[3,32,16,128]{3,2,1,0:T(8,128)}, u32[]{:S(2)}) %copy-start.2) | copy-done | bytes 786456
  3.7 0.0 copy-start.3
  3.7 0.9 %copy-done.3 = f32[32,16,128]{2,1,0:T(8,128)S(1)} copy-done((f32[32,16,128]{2,1,0:T(8,128)S(1)}, f32[32,16,128]{2,1,0:T(8,128)}, u32[]{:S(2)}) %copy-start.3) | copy-done | bytes 262168
  4.6 0.0 copy-start.4
  4.6 0.9 %copy-done.4 = s32[32,16,128]{2,1,0:T(8,128)S(1)} copy-done((s32[32,16,128]{2,1,0:T(8,128)S(1)}, s32[32,16,128]{2,1,0:T(8,128)}, u32[]{:S(2)}) %copy-start.4) | copy-done | bytes 262168
  5.6 41.7 %shard_map.55 = f32[6,512,128]{2,1,0:T(8,128)S(1)} custom-call(f32[6,512,128]{2,1,0:T(8,128)S(1)} %bitcast.7, f32[512,128]{1,0:T(8,128)S(1)} %bitcast.10, s32[512,128]{1,0:T(8,128)S(1)} %bitcast.11, f32[3,512,128]{2,1,0:T(8,128)S(1)} %bitcast.8, s32[3,512,128]{2,1,0:T(8,128)S(1)} %bitcast.9), custom_call_target="tpu_custom_call" | custom-call | tf_op jit(solution)/shard_map/pallas_call | solution.py:578
  47.2 1.1 %copy.7 = f32[6,32,16,128]{3,2,1,0:T(8,128)} copy(f32[6,32,16,128]{3,2,1,0:T(8,128)S(1)} %bitcast.6) | data formatting | bytes 3145728
Async XLA Ops:
  0.0 1.4 %copy-start = (f32[6,32,16,128]{3,2,1,0:T(8,128)S(1)}, f32[6,32,16,128]{3,2,1,0:T(8,128)}, u32[]{:S(2)}) copy-start(f32[6,32,16,128]{3,2,1,0:T(8,128)} %param.5) | copy-start | bytes 4718596
  1.4 1.1 %copy-start.1 = (f32[3,32,16,128]{3,2,1,0:T(8,128)S(1)}, f32[3,32,16,128]{3,2,1,0:T(8,128)}, u32[]{:S(2)}) copy-start(f32[3,32,16,128]{3,2,1,0:T(8,128)} %param.8) | copy-start | bytes 2359300
  2.5 1.1 %copy-start.2 = (s32[3,32,16,128]{3,2,1,0:T(8,128)S(1)}, s32[3,32,16,128]{3,2,1,0:T(8,128)}, u32[]{:S(2)}) copy-start(s32[3,32,16,128]{3,2,1,0:T(8,128)} %param.9) | copy-start | bytes 2359300
  3.7 0.9 %copy-start.3 = (f32[32,16,128]{2,1,0:T(8,128)S(1)}, f32[32,16,128]{2,1,0:T(8,128)}, u32[]{:S(2)}) copy-start(f32[32,16,128]{2,1,0:T(8,128)} %param.6) | copy-start | bytes 786436
  4.6 0.9 %copy-start.4 = (s32[32,16,128]{2,1,0:T(8,128)S(1)}, s32[32,16,128]{2,1,0:T(8,128)}, u32[]{:S(2)}) copy-start(s32[32,16,128]{2,1,0:T(8,128)} %param.7) | copy-start | bytes 786436
where the time goes:
time: 48.7 us; the launch traced here: 48.4 us
  Pallas kernels  41.7 us (86%)
  local copies, waits for them, and re-layouts  6.72 us (14%)
    pallas_call x1, Pallas kernels, on_device(): pl.pallas_call(body, out_shape=jax.ShapeDtypeStruct((C, LINES, Z), f32),...  41.7 us
    unnamed x11, local copies, waits for them, and re-layouts  6.72 us

commit v1 on v0

--- a/solution.py
+++ b/solution.py
@@ -26,16 +26,16 @@
 
 
 def body(
-    cot_h, dif_h, pha_h, cou_h, upw_h, out_h,
+    cot_h, dif_h, pha_h, cou_h, upw_h, out,
     cot, dif, pha, cou, upw, ec,
-    zt, zw, zo, zb, tri,
+    et, zt, zw, zo, zb, tri,
     yb, ya, yw, yo, yr, yf, ay, ayh,
     xe, xb, xa, xw, xo, xr,
     csy, csx, rcy, rcx, ky, kx, gl,
     sty, tty, oty, rty, stx, ttx, otx, rtx, ext,
     fsy, fry, fsx, frx,
     c0, ax, bx, ayp, byp, azn, bzp, fb,
-    in_sem, out_sem,
+    in_sem,
     s_cy, r_cy, s_cx, r_cx, s_fy, r_fy, s_fx, r_fx,
     s_ty, r_ty, s_oy, r_oy, s_tx, r_tx, s_ox, r_ox, s_ex, r_ex,
 ):
@@ -241,34 +241,55 @@
     for f in faces:
         f.start()
 
-    lane = lax.broadcasted_iota(jnp.int32, (64, Z), 1)
-
-    def z_factor(block, _):
-        rows = pl.ds(pl.multiple_of(block * 64, 64), 64)
-        e = ec[rows, :]
-        p11, p12, p21, p22 = 1.0 + e, jnp.ones_like(e), e, jnp.ones_like(e)
-        step = 1
-        while step < Z:
-            keep = lane < step
-            q11 = jnp.where(keep, 1.0, pltpu.roll(p11, step, 1))
-            q12 = jnp.where(keep, 0.0, pltpu.roll(p12, step, 1))
-            q21 = jnp.where(keep, 0.0, pltpu.roll(p21, step, 1))
-            q22 = jnp.where(keep, 1.0, pltpu.roll(p22, step, 1))
+    seg = lax.broadcasted_iota(jnp.int32, (8, Z), 0)
+    span = Z // 8
+    tiles = LINES // Z
+    for t in range(tiles):
+        et[t] = ec[t * Z : (t + 1) * Z, :].T
+    ones = jnp.ones((8, Z), f32)
+    zeros = jnp.zeros((8, Z), f32)
+
+    def cell(t, step):
+        return et[t, pl.ds(step, 8, stride=span), :]
+
+    starts = []
+    for t in range(tiles):
+        p11, p12, p21, p22 = ones, zeros, zeros, ones
+        for step in range(span):
+            e = cell(t, step)
+            p21 = p21 + e * p11
+            p22 = p22 + e * p12
+            p11 = p11 + p21
+            p12 = p12 + p22
+        for shift in (1, 2, 4):
+            keep = seg < shift
+            q11 = jnp.where(keep, 1.0, pltpu.roll(p11, shift, 0))
+            q12 = jnp.where(keep, 0.0, pltpu.roll(p12, shift, 0))
+            q21 = jnp.where(keep, 0.0, pltpu.roll(p21, shift, 0))
+            q22 = jnp.where(keep, 1.0, pltpu.roll(p22, shift, 0))
             p11, p12, p21, p22 = (
                 p11 * q11 + p12 * q21,
                 p11 * q12 + p12 * q22,
                 p21 * q11 + p22 * q21,
                 p21 * q12 + p22 * q22,
             )
-            step *= 2
-        theta = p11 + p12
+        theta = jnp.where(seg < 1, 1.0, pltpu.roll(p11 + p12, 1, 0))
+        delta = jnp.where(seg < 1, 1.0, pltpu.roll(p21 + p22, 1, 0))
+        starts.append((theta, delta))
+    for t in range(tiles):
+        theta, delta = starts[t]
+        for step in range(span):
+            delta = delta + cell(t, step) * theta
+            theta = theta + delta
+            et[t, pl.ds(step, 8, stride=span), :] = theta
+    lane = lax.broadcasted_iota(jnp.int32, (Z, Z), 1)
+    for t in range(tiles):
+        rows = pl.ds(t * Z, Z)
+        theta = et[t].T
         before = jnp.where(lane < 1, 1.0, pltpu.roll(theta, 1, 1))
         zt[rows, :] = before
         zw[rows, :] = 1.0 / (theta * before)
-        zo[rows, :] = before * e
-        return 0
-
-    lax.fori_loop(0, LINES // 64, z_factor, 0)
+        zo[rows, :] = before * ec[rows, :]
 
     row = lax.rem(lax.broadcasted_iota(jnp.int32, (2 * Z, Z), 0), Z)
     col = lax.broadcasted_iota(jnp.int32, (2 * Z, Z), 1)
@@ -525,16 +546,10 @@
             result -= from_y * fb[pl.ds(at - 1, Y), :]
             result += to_z * pltpu.roll(value, Z - 1, 1)
             result -= from_z * pltpu.roll(value, 1, 1)
-            cot[c, rows, :] = result
+            out[c, rows, :] = result
         return 0
 
-    stores = []
-    for part in range(4):
-        lax.fori_loop(part * 8, part * 8 + 8, advect, 0, unroll=2)
-        rows = pl.ds(part * 8 * Y, 8 * Y)
-        store = pltpu.make_async_copy(cot.at[:, rows, :], out_h.at[:, rows, :], out_sem.at[part])
-        store.start()
-        stores.append(store)
+    lax.fori_loop(0, X, advect, 0, unroll=2)
 
     sent_all(*tot_x)
     sent_all(*ret_x)
@@ -549,9 +564,6 @@
         for m in range(NI):
             extra(m, 0, jnext).wait_send()
 
-    for store in stores:
-        store.wait()
-
 
 def on_device(cotangent, diffusion, phase, courant, upwind):
     def vm(*shape, dtype=f32):
@@ -561,7 +573,7 @@
     scratch = [
         vm(C, LINES, Z), vm(LINES, Z), vm(LINES, Z, dtype=jnp.int32), vm(3, LINES, Z), vm(3, LINES, Z, dtype=jnp.int32),
         vm(LINES, Z),
-        vm(LINES, Z), vm(LINES, Z), vm(LINES, Z), vm(C, LINES, Z), vm(2, 2 * Z, Z, dtype=jnp.bfloat16),
+        vm(LINES // Z, Z, Z), vm(LINES, Z), vm(LINES, Z), vm(LINES, Z), vm(C, LINES, Z), vm(2, 2 * Z, Z, dtype=jnp.bfloat16),
         vm(Y, X, Z), vm(Y, X, Z), vm(Y, X, Z), vm(Y, X, Z), vm(X, Z), vm(C, Y, X, Z), vm(C, LINES, Z), vm(X * 16, Z),
         vm(X, 32, Z), vm(X, 32, Z), vm(X, 32, Z), vm(X, 32, Z), vm(X, 32, Z), vm(32, Z),
         vm(NJ * 8, Z), vm(NI * 8, Z), vm(NJ * 8, Z), vm(NI * 8, Z), vm(6, NJ, 16, Z), vm(6, NI, 16, Z), vm(2, NJ, 16, Z),
@@ -570,7 +582,7 @@
         vm(2, 2, X, Z), vm(2, 2, X, Z), vm(2, Y, Z), vm(2, Y, Z),
         vm(LINES, Z), vm(LINES + 2 * Y, Z), vm(LINES + 2 * Y, Z), vm(X * PAD + 8, Z), vm(X * PAD + 8, Z), vm(LINES, Z), vm(LINES, Z),
         vm(8 * PITCH, Z),
-        dma((5,)), dma((4,)),
+        dma((5,)),
         dma((NJ,)), dma((NJ,)), dma((NI,)), dma((NI,)), dma((2,)), dma((2,)), dma((2,)), dma((2,)),
         dma((NJ,)), dma((NJ,)), dma((NJ,)), dma((NJ,)), dma((NI,)), dma((NI,)), dma((NI,)), dma((NI,)),
         dma((2, NI)), dma((2,)),
@@ -578,18 +590,23 @@
     out = pl.pallas_call(
         body,
         out_shape=jax.ShapeDtypeStruct((C, LINES, Z), f32),
-        in_specs=[pl.BlockSpec(memory_space=pl.ANY)] * 5,
-        out_specs=pl.BlockSpec(memory_space=pl.ANY),
+        in_specs=[pl.BlockSpec(memory_space=pltpu.HBM)] * 5,
+        out_specs=pl.BlockSpec(memory_space=pltpu.VMEM),
         scratch_shapes=scratch,
         compiler_params=pltpu.CompilerParams(
             collective_id=0, has_side_effects=True, vmem_limit_bytes=48 * 1024 * 1024
         ),
     )(
-        cotangent.reshape(C, LINES, Z),
-        diffusion.reshape(LINES, Z),
-        phase.reshape(LINES, Z),
-        courant.reshape(3, LINES, Z),
-        upwind.reshape(3, LINES, Z),
+        *(
+            pltpu.with_memory_space_constraint(given, pltpu.HBM)
+            for given in (
+                cotangent.reshape(C, LINES, Z),
+                diffusion.reshape(LINES, Z),
+                phase.reshape(LINES, Z),
+                courant.reshape(3, LINES, Z),
+                upwind.reshape(3, LINES, Z),
+            )
+        )
     )
     return out.reshape(C, X, Y, Z)
 

time: 48.7 us -> 37 us (0.76)
  Pallas kernels: 41.7 us -> 35.8 us
  local copies, waits for them, and re-layouts: 6.72 us -> 1.15 us
    pallas_call x1, Pallas kernels: 41.7 us -> 35.8 us  [on_device(): pl.pallas_call(body, out_shape=jax.ShapeDtypeStruct((C, LINES, Z), f32),...]
    unnamed x11 -> x1, local copies, waits for them, and re-layouts: 6.72 us -> 1.15 us
where the time goes in v1:
time: 37 us; the launch traced here: 36.9 us
  Pallas kernels  35.8 us (97%)
  local copies, waits for them, and re-layouts  1.15 us (3%)
    pallas_call x1, Pallas kernels, on_device(): pl.pallas_call(body, out_shape=jax.ShapeDtypeStruct((C, LINES, Z), f32),...  35.8 us
    unnamed x1, local copies, waits for them, and re-layouts  1.15 us

profile of v1, /device:TPU:1, one launch (start us, length us, event | category | flops | bytes accessed | tf_op | source)
XLA Modules:
  0.0 36.9 jit_solution(6420085259688602471)
XLA Ops:
  0.0 35.8 %shard_map.55 = f32[6,512,128]{2,1,0:T(8,128)S(1)} custom-call(f32[6,512,128]{2,1,0:T(8,128)} %bitcast.7, f32[512,128]{1,0:T(8,128)} %bitcast.10, s32[512,128]{1,0:T(8,128)} %bitcast.11, f32[3,512,128]{2,1,0:T(8,128)} %bitcast.8, s32[3,512,128]{2,1,0:T(8,128)} %bitcast.9), custom_call_target="tpu_custom_call" | custom-call | tf_op jit(solution)/shard_map/pallas_call | solution.py:590
  35.8 1.1 %copy.7 = f32[6,32,16,128]{3,2,1,0:T(8,128)} copy(f32[6,32,16,128]{3,2,1,0:T(8,128)S(1)} %bitcast.6) | data formatting | bytes 3145728

commit v2 on v1

--- a/solution.py
+++ b/solution.py
@@ -33,10 +33,10 @@
     xe, xb, xa, xw, xo, xr,
     csy, csx, rcy, rcx, ky, kx, gl,
     sty, tty, oty, rty, stx, ttx, otx, rtx, ext,
-    fsy, fry, fsx, frx,
+    fse, fre, fsy, fry, fsx, frx,
     c0, ax, bx, ayp, byp, azn, bzp, fb,
     in_sem,
-    s_cy, r_cy, s_cx, r_cx, s_fy, r_fy, s_fx, r_fx,
+    s_cy, r_cy, s_cx, r_cx, s_fe, r_fe, s_fy, r_fy, s_fx, r_fx,
     s_ty, r_ty, s_oy, r_oy, s_tx, r_tx, s_ox, r_ox, s_ex, r_ex,
 ):
     i = lax.axis_index("gx")
@@ -51,7 +51,7 @@
         pltpu.make_async_copy(cou_h, cou, in_sem.at[3]),
         pltpu.make_async_copy(upw_h, upw, in_sem.at[4]),
     ]
-    for load in loads:
+    for load in loads[:3]:
         load.start()
 
     barrier = pltpu.get_barrier_semaphore()
@@ -109,137 +109,6 @@
             delta = delta + cells[y] * phi
             phi = phi + delta
         csy[pl.ds(at + 2, 8, stride=8), :] = rn
-
-    def x_factor(lo):
-        rows = pl.ds(lo, 16)
-        one = jnp.ones((16, Z), f32)
-
-        def up(x, carry):
-            theta, delta = carry
-            xb[x, rows, :] = theta
-            delta = delta + xe[x, rows, :] * theta
-            return theta + delta, delta
-
-        theta, _ = lax.fori_loop(0, X, up, (one, one), unroll=8)
-        rn = 1.0 / theta
-        xr[rows, :] = rn
-
-        def down(step, carry):
-            x = X - 1 - step
-            phi, delta, after, _ = carry
-            cell = xe[x, rows, :]
-            a = phi * rn
-            b = xb[x, rows, :] * rn
-            xa[x, rows, :] = a
-            xb[x, rows, :] = b
-            xw[x, rows, :] = 1.0 / (b * after)
-            xo[x, rows, :] = b * cell
-            delta = delta + cell * phi
-            return phi + delta, delta, b, a
-
-        _, _, _, first = lax.fori_loop(0, X, down, (one, one, one, one), unroll=8)
-        return first, rn
-
-    for x in range(X):
-        xe[x, 0:Y, :] = ec[x * Y : (x + 1) * Y, :]
-    first, rn = x_factor(0)
-    last = xb[X - 1, 0:Y, :]
-    for r in range(2):
-        csx[pl.ds(r, 8, stride=8), :] = first[r * 8 : r * 8 + 8]
-        csx[pl.ds(2 + r, 8, stride=8), :] = rn[r * 8 : r * 8 + 8]
-        csx[pl.ds(4 + r, 8, stride=8), :] = last[r * 8 : r * 8 + 8]
-
-    loads[3].wait()
-    loads[4].wait()
-    fsy[0, 0] = ec[pl.ds(0, X, stride=Y), :]
-    fsy[1, 0] = ec[pl.ds(Y - 1, X, stride=Y), :]
-    fsy[0, 1] = upw[1, pl.ds(0, X, stride=Y), :].astype(f32) * cou[1, pl.ds(0, X, stride=Y), :]
-    fsy[1, 1] = (1.0 - upw[1, pl.ds(Y - 1, X, stride=Y), :].astype(f32)) * cou[1, pl.ds(Y - 1, X, stride=Y), :]
-    fsx[0] = upw[0, 0:Y, :].astype(f32) * cou[0, 0:Y, :] * ec[0:Y, :]
-    fsx[1] = (1.0 - upw[0, LINES - Y : LINES, :].astype(f32)) * cou[0, LINES - Y : LINES, :] * ec[LINES - Y : LINES, :]
-
-    outer = (i == 0) | (i == NI - 1)
-    pl.semaphore_wait(barrier, NI + NJ - 2 + jnp.where(outer, NI - 1, 0))
-
-    def exchange(src, dst, send, recv, rows, k, axis):
-        here = j if axis == "gy" else i
-        return pltpu.make_async_remote_copy(
-            src_ref=src.at[pl.ds(pl.multiple_of(k * rows, 8), rows), :],
-            dst_ref=dst.at[pl.ds(pl.multiple_of(here * rows, 8), rows), :],
-            send_sem=send.at[k],
-            recv_sem=recv.at[here],
-            device_id={axis: k},
-            device_id_type=MESH,
-        )
-
-    def arrival(src, dst, send, recv, rows, k, axis):
-        return pltpu.make_async_remote_copy(
-            src_ref=src.at[pl.ds(pl.multiple_of(k * rows, 8), rows), :],
-            dst_ref=dst.at[pl.ds(pl.multiple_of(k * rows, 8), rows), :],
-            send_sem=send.at[k],
-            recv_sem=recv.at[k],
-            device_id={axis: k},
-            device_id_type=MESH,
-        )
-
-    def count_of(axis):
-        return NJ if axis == "gy" else NI
-
-    def send_all(src, dst, send, recv, rows, axis):
-        n = count_of(axis)
-        here = j if axis == "gy" else i
-        mine = pl.ds(pl.multiple_of(here * rows, 8), rows)
-
-        def step(d, _):
-            exchange(src, dst, send, recv, rows, lax.rem(here + d, n), axis).start()
-            return 0
-
-        lax.fori_loop(1, n, step, 0)
-        dst[mine, :] = src[mine, :]
-
-    def recv_all(src, dst, send, recv, rows, axis):
-        n = count_of(axis)
-        here = j if axis == "gy" else i
-
-        def step(d, _):
-            arrival(src, dst, send, recv, rows, lax.rem(here + d, n), axis).wait_recv()
-            return 0
-
-        lax.fori_loop(1, n, step, 0)
-
-    def sent_all(src, dst, send, recv, rows, axis):
-        n = count_of(axis)
-        here = j if axis == "gy" else i
-
-        def step(d, _):
-            arrival(src, dst, send, recv, rows, lax.rem(here + d, n), axis).wait_send()
-            return 0
-
-        lax.fori_loop(1, n, step, 0)
-
-    coup_y = (csy, rcy, s_cy, r_cy, 8, "gy")
-    coup_x = (csx, rcx, s_cx, r_cx, 8, "gx")
-    tot_y = (sty, tty, s_ty, r_ty, PACK, "gy")
-    ret_y = (oty, rty, s_oy, r_oy, PACK, "gy")
-    tot_x = (stx, ttx, s_tx, r_tx, PACK, "gx")
-    ret_x = (otx, rtx, s_ox, r_ox, PACK, "gx")
-
-    def face(src, dst, send, recv, slot, axis, to):
-        return pltpu.make_async_remote_copy(
-            src_ref=src.at[slot], dst_ref=dst.at[slot], send_sem=send.at[slot], recv_sem=recv.at[slot],
-            device_id={axis: to}, device_id_type=MESH,
-        )
-
-    faces = [
-        face(fsy, fry, s_fy, r_fy, 0, "gy", jprev),
-        face(fsy, fry, s_fy, r_fy, 1, "gy", jnext),
-        face(fsx, frx, s_fx, r_fx, 0, "gx", iprev),
-        face(fsx, frx, s_fx, r_fx, 1, "gx", inext),
-    ]
-    send_all(*coup_y)
-    send_all(*coup_x)
-    for f in faces:
-        f.start()
 
     seg = lax.broadcasted_iota(jnp.int32, (8, Z), 0)
     span = Z // 8
@@ -296,7 +165,96 @@
     tri[0] = (row <= col).astype(f32).astype(jnp.bfloat16)
     tri[1] = (row >= col).astype(f32).astype(jnp.bfloat16)
 
+    outer = (i == 0) | (i == NI - 1)
+    pl.semaphore_wait(barrier, NI + NJ - 2 + jnp.where(outer, NI - 1, 0))
+
+    def exchange(src, dst, send, recv, rows, k, axis):
+        here = j if axis == "gy" else i
+        return pltpu.make_async_remote_copy(
+            src_ref=src.at[pl.ds(pl.multiple_of(k * rows, 8), rows), :],
+            dst_ref=dst.at[pl.ds(pl.multiple_of(here * rows, 8), rows), :],
+            send_sem=send.at[k],
+            recv_sem=recv.at[here],
+            device_id={axis: k},
+            device_id_type=MESH,
+        )
+
+    def arrival(src, dst, send, recv, rows, k, axis):
+        return pltpu.make_async_remote_copy(
+            src_ref=src.at[pl.ds(pl.multiple_of(k * rows, 8), rows), :],
+            dst_ref=dst.at[pl.ds(pl.multiple_of(k * rows, 8), rows), :],
+            send_sem=send.at[k],
+            recv_sem=recv.at[k],
+            device_id={axis: k},
+            device_id_type=MESH,
+        )
+
+    def count_of(axis):
+        return NJ if axis == "gy" else NI
+
+    def send_all(src, dst, send, recv, rows, axis):
+        n = count_of(axis)
+        here = j if axis == "gy" else i
+        mine = pl.ds(pl.multiple_of(here * rows, 8), rows)
+
+        def step(d, _):
+            exchange(src, dst, send, recv, rows, lax.rem(here + d, n), axis).start()
+            return 0
+
+        lax.fori_loop(1, n, step, 0)
+        dst[mine, :] = src[mine, :]
+
+    def recv_all(src, dst, send, recv, rows, axis):
+        n = count_of(axis)
+        here = j if axis == "gy" else i
+
+        def step(d, _):
+            arrival(src, dst, send, recv, rows, lax.rem(here + d, n), axis).wait_recv()
+            return 0
+
+        lax.fori_loop(1, n, step, 0)
+
+    def sent_all(src, dst, send, recv, rows, axis):
+        n = count_of(axis)
+        here = j if axis == "gy" else i
+
+        def step(d, _):
+            arrival(src, dst, send, recv, rows, lax.rem(here + d, n), axis).wait_send()
+            return 0
+
+        lax.fori_loop(1, n, step, 0)
+
+    coup_y = (csy, rcy, s_cy, r_cy, 8, "gy")
+    coup_x = (csx, rcx, s_cx, r_cx, 8, "gx")
+    tot_y = (sty, tty, s_ty, r_ty, PACK, "gy")
+    ret_y = (oty, rty, s_oy, r_oy, PACK, "gy")
+    tot_x = (stx, ttx, s_tx, r_tx, PACK, "gx")
+    ret_x = (otx, rtx, s_ox, r_ox, PACK, "gx")
+
+    def face(src, dst, send, recv, slot, axis, to):
+        return pltpu.make_async_remote_copy(
+            src_ref=src.at[slot], dst_ref=dst.at[slot], send_sem=send.at[slot], recv_sem=recv.at[slot],
+            device_id={axis: to}, device_id_type=MESH,
+        )
+
+    edges = [
+        face(fse, fre, s_fe, r_fe, 0, "gy", jprev),
+        face(fse, fre, s_fe, r_fe, 1, "gy", jnext),
+    ]
+    faces = [
+        face(fsy, fry, s_fy, r_fy, 0, "gy", jprev),
+        face(fsy, fry, s_fy, r_fy, 1, "gy", jnext),
+        face(fsx, frx, s_fx, r_fx, 0, "gx", iprev),
+        face(fsx, frx, s_fx, r_fx, 1, "gx", inext),
+    ]
+    send_all(*coup_y)
+    fse[0] = ec[pl.ds(0, X, stride=Y), :]
+    fse[1] = ec[pl.ds(Y - 1, X, stride=Y), :]
+    for e in edges:
+        e.start()
     loads[2].wait()
+    loads[3].start()
+    loads[4].start()
 
     def z_and_y(q):
         rows = pl.ds(q * 8 * Y, 8 * Y)
@@ -343,6 +301,60 @@
     mine_y = pl.ds(pl.multiple_of(j * PACK, 8), PACK)
     tty[mine_y, :] = sty[mine_y, :]
 
+    def x_factor():
+        rows = pl.ds(0, 32)
+        one = jnp.ones((32, Z), f32)
+
+        def up(x, carry):
+            theta, delta = carry
+            xb[x, rows, :] = theta
+            delta = delta + xe[x, rows, :] * theta
+            return theta + delta, delta
+
+        theta, _ = lax.fori_loop(0, X, up, (one, one), unroll=8)
+        rn = 1.0 / theta
+        xr[rows, :] = rn
+
+        def down(step, carry):
+            x = X - 1 - step
+            phi, delta, after, _ = carry
+            cell = xe[x, rows, :]
+            a = phi * rn
+            b = xb[x, rows, :] * rn
+            xa[x, rows, :] = a
+            xb[x, rows, :] = b
+            xw[x, rows, :] = 1.0 / (b * after)
+            xo[x, rows, :] = b * cell
+            delta = delta + cell * phi
+            return phi + delta, delta, b, a
+
+        _, _, _, first = lax.fori_loop(0, X, down, (one, one, one, one), unroll=8)
+        return first, rn
+
+    for e in edges:
+        e.wait_recv()
+    for x in range(X):
+        xe[x, 0:Y, :] = ec[x * Y : (x + 1) * Y, :]
+        xe[x, 16:24, :] = jnp.broadcast_to(fre[1, x : x + 1, :], (8, Z))
+        xe[x, 24:32, :] = jnp.broadcast_to(fre[0, x : x + 1, :], (8, Z))
+    first, rn = x_factor()
+    last = xb[X - 1, 0:Y, :]
+    for r in range(2):
+        csx[pl.ds(r, 8, stride=8), :] = first[r * 8 : r * 8 + 8]
+        csx[pl.ds(2 + r, 8, stride=8), :] = rn[r * 8 : r * 8 + 8]
+        csx[pl.ds(4 + r, 8, stride=8), :] = last[r * 8 : r * 8 + 8]
+
+    loads[3].wait()
+    loads[4].wait()
+    fsy[0] = upw[1, pl.ds(0, X, stride=Y), :].astype(f32) * cou[1, pl.ds(0, X, stride=Y), :]
+    fsy[1] = (1.0 - upw[1, pl.ds(Y - 1, X, stride=Y), :].astype(f32)) * cou[1, pl.ds(Y - 1, X, stride=Y), :]
+    fsx[0] = upw[0, 0:Y, :].astype(f32) * cou[0, 0:Y, :] * ec[0:Y, :]
+    fsx[1] = (1.0 - upw[0, LINES - Y : LINES, :].astype(f32)) * cou[0, LINES - Y : LINES, :] * ec[LINES - Y : LINES, :]
+
+    send_all(*coup_x)
+    for f in faces:
+        f.start()
+
     def reduce_factor(count, couplings, factors):
         def pair(base, t):
             return jnp.concatenate(
@@ -393,11 +405,6 @@
     reduce_factor(NI, rcx, kx)
     for f in faces:
         f.wait_recv()
-
-    for x in range(X):
-        xe[x, 16:24, :] = jnp.broadcast_to(fry[1, 0, x : x + 1, :], (8, Z))
-        xe[x, 24:32, :] = jnp.broadcast_to(fry[0, 0, x : x + 1, :], (8, Z))
-    x_factor(16)
 
     low_ok = jnp.where(j > 0, 1.0, 0.0).astype(f32)
     high_ok = jnp.where(j < NJ - 1, 1.0, 0.0).astype(f32)
@@ -419,11 +426,11 @@
         bzp[rows, :] = jnp.where(lane16 > 0, pltpu.roll(behind[2], 1, 1), 0.0)
         return 0
 
-    lax.fori_loop(0, X, coefficients, 0, unroll=2)
+    lax.fori_loop(0, X, coefficients, 0, unroll=8)
     bx[0:Y, :] = frx[1]
     ax[(X + 1) * Y : (X + 2) * Y, :] = frx[0]
-    byp[pl.ds(7, X, stride=PAD), :] = fry[1, 1] * low_ok
-    ayp[pl.ds(PAD, X, stride=PAD), :] = fry[0, 1] * high_ok
+    byp[pl.ds(7, X, stride=PAD), :] = fry[1] * low_ok
+    ayp[pl.ds(PAD, X, stride=PAD), :] = fry[0] * high_ok
     ayh[...] = jnp.zeros_like(ayh)
 
     recv_all(*ret_y)
@@ -435,8 +442,8 @@
         for c in range(C):
             left = rty[pl.ds(at + c, 8, stride=PACK), :]
             right = rty[pl.ds(at + HALF + c, 8, stride=PACK), :]
-            ayh[pl.ds(q * 8 * 16 + c, 8, stride=16), :] = left * fry[1, 0, xs, :]
-            ayh[pl.ds(q * 8 * 16 + 8 + c, 8, stride=16), :] = right * fry[0, 0, xs, :]
+            ayh[pl.ds(q * 8 * 16 + c, 8, stride=16), :] = left * fre[1, xs, :]
+            ayh[pl.ds(q * 8 * 16 + 8 + c, 8, stride=16), :] = right * fre[0, xs, :]
             below.append(left * yr[xs, :])
             live.append(right)
         for y in range(Y - 1, -1, -1):
@@ -461,7 +468,7 @@
         return tuple(new_heads), tuple(new_tails), halo
 
     none = jnp.zeros((Y, Z), f32)
-    heads, tails, _ = lax.fori_loop(0, X, x_totals, ((none,) * C, (none,) * C, none), unroll=2)
+    heads, tails, _ = lax.fori_loop(0, X, x_totals, ((none,) * C, (none,) * C, none), unroll=8)
     for c in range(C):
         for r in range(2):
             stx[pl.ds(r * C + c, 8, stride=PACK), :] = heads[c][r * 8 : r * 8 + 8]
@@ -471,7 +478,7 @@
     sent_all(*coup_x)
     sent_all(*tot_y)
     sent_all(*ret_y)
-    for f in faces:
+    for f in edges + faces:
         f.wait_send()
     recv_all(*tot_x)
     reduce_solve(NI, ttx, kx, otx)
@@ -528,7 +535,7 @@
         fb[pl.ds((x + 2) * PAD, 8, stride=PITCH), :] = edge[8:16]
         return tuple(out), halo
 
-    lax.fori_loop(0, X, x_finish, (tuple(rights), right_halo), unroll=2)
+    lax.fori_loop(0, X, x_finish, (tuple(rights), right_halo), unroll=4)
 
     def advect(x, _):
         rows = pl.ds(pl.multiple_of(x * Y, Y), Y)
@@ -549,7 +556,7 @@
             out[c, rows, :] = result
         return 0
 
-    lax.fori_loop(0, X, advect, 0, unroll=2)
+    lax.fori_loop(0, X, advect, 0, unroll=8)
 
     sent_all(*tot_x)
     sent_all(*ret_x)
@@ -579,11 +586,11 @@
         vm(NJ * 8, Z), vm(NI * 8, Z), vm(NJ * 8, Z), vm(NI * 8, Z), vm(6, NJ, 16, Z), vm(6, NI, 16, Z), vm(2, NJ, 16, Z),
         vm(NJ * PACK, Z), vm(NJ * PACK, Z), vm(NJ * PACK, Z), vm(NJ * PACK, Z),
         vm(NI * PACK, Z), vm(NI * PACK, Z), vm(NI * PACK, Z), vm(NI * PACK, Z), vm(2, 32, Z),
-        vm(2, 2, X, Z), vm(2, 2, X, Z), vm(2, Y, Z), vm(2, Y, Z),
+        vm(2, X, Z), vm(2, X, Z), vm(2, X, Z), vm(2, X, Z), vm(2, Y, Z), vm(2, Y, Z),
         vm(LINES, Z), vm(LINES + 2 * Y, Z), vm(LINES + 2 * Y, Z), vm(X * PAD + 8, Z), vm(X * PAD + 8, Z), vm(LINES, Z), vm(LINES, Z),
         vm(8 * PITCH, Z),
         dma((5,)),
-        dma((NJ,)), dma((NJ,)), dma((NI,)), dma((NI,)), dma((2,)), dma((2,)), dma((2,)), dma((2,)),
+        dma((NJ,)), dma((NJ,)), dma((NI,)), dma((NI,)), dma((2,)), dma((2,)), dma((2,)), dma((2,)), dma((2,)), dma((2,)),
         dma((NJ,)), dma((NJ,)), dma((NJ,)), dma((NJ,)), dma((NI,)), dma((NI,)), dma((NI,)), dma((NI,)),
         dma((2, NI)), dma((2,)),
     ]

time: 37 us -> 35.3 us (0.954)
  Pallas kernels: 35.8 us -> 34 us
    pallas_call x1, Pallas kernels: 35.8 us -> 34 us  [on_device(): pl.pallas_call(body, out_shape=jax.ShapeDtypeStruct((C, LINES, Z), f32),...]
where the time goes in v2:
time: 35.3 us; the launch traced here: 35.2 us
  Pallas kernels  34 us (96%)
  local copies, waits for them, and re-layouts  1.15 us (3%)
    pallas_call x1, Pallas kernels, on_device(): pl.pallas_call(body, out_shape=jax.ShapeDtypeStruct((C, LINES, Z), f32),...  34 us
    unnamed x1, local copies, waits for them, and re-layouts  1.15 us

profile of v2, /device:TPU:1, one launch (start us, length us, event | category | flops | bytes accessed | tf_op | source)
XLA Modules:
  0.0 35.2 jit_solution(449306003791076670)
XLA Ops:
  0.0 34.0 %shard_map.55 = f32[6,512,128]{2,1,0:T(8,128)S(1)} custom-call(f32[6,512,128]{2,1,0:T(8,128)} %bitcast.7, f32[512,128]{1,0:T(8,128)} %bitcast.10, s32[512,128]{1,0:T(8,128)} %bitcast.11, f32[3,512,128]{2,1,0:T(8,128)} %bitcast.8, s32[3,512,128]{2,1,0:T(8,128)} %bitcast.9), custom_call_target="tpu_custom_call" | custom-call | tf_op jit(solution)/shard_map/pallas_call | solution.py:597
  34.0 1.1 %copy.7 = f32[6,32,16,128]{3,2,1,0:T(8,128)} copy(f32[6,32,16,128]{3,2,1,0:T(8,128)S(1)} %bitcast.6) | data formatting | bytes 3145728

commit v3 on v2

--- a/solution.py
+++ b/solution.py
@@ -17,6 +17,8 @@
 HALF = C * 2
 PACK = 2 * HALF
 f32 = jnp.float32
+FAR = sorted(((a, b) for a in range(4) for b in range(4) if a or b), key=lambda d: -min(d[0], 4 - d[0]) - min(d[1], 4 - d[1]))
+FAR_X = [(2, 1), (2, 0), (3, 1), (1, 1), (3, 0), (1, 0), (0, 1)]
 
 
 def split(values):
@@ -26,7 +28,8 @@
 
 
 def body(
-    cot_h, dif_h, pha_h, cou_h, upw_h, out,
+    cot_h, dif_h, pha_h, cou_h, upw_h,
+    fb, c0, ax, bx, ayp, byp, azn, bzp,
     cot, dif, pha, cou, upw, ec,
     et, zt, zw, zo, zb, tri,
     yb, ya, yw, yo, yr, yf, ay, ayh,
@@ -34,7 +37,6 @@
     csy, csx, rcy, rcx, ky, kx, gl,
     sty, tty, oty, rty, stx, ttx, otx, rtx, ext,
     fse, fre, fsy, fry, fsx, frx,
-    c0, ax, bx, ayp, byp, azn, bzp, fb,
     in_sem,
     s_cy, r_cy, s_cx, r_cx, s_fe, r_fe, s_fy, r_fy, s_fx, r_fx,
     s_ty, r_ty, s_oy, r_oy, s_tx, r_tx, s_ox, r_ox, s_ex, r_ex,
@@ -189,40 +191,25 @@
             device_id_type=MESH,
         )
 
-    def count_of(axis):
-        return NJ if axis == "gy" else NI
+    def peers(axis):
+        if axis == "gy":
+            return [lax.rem(j // 4 + a, 4) * 4 + lax.rem(j + b, 4) for a, b in FAR]
+        return [lax.rem(i // 2 + a, 4) * 2 + lax.rem(i + b, 2) for a, b in FAR_X]
 
     def send_all(src, dst, send, recv, rows, axis):
-        n = count_of(axis)
         here = j if axis == "gy" else i
         mine = pl.ds(pl.multiple_of(here * rows, 8), rows)
-
-        def step(d, _):
-            exchange(src, dst, send, recv, rows, lax.rem(here + d, n), axis).start()
-            return 0
-
-        lax.fori_loop(1, n, step, 0)
+        for k in peers(axis):
+            exchange(src, dst, send, recv, rows, k, axis).start()
         dst[mine, :] = src[mine, :]
 
     def recv_all(src, dst, send, recv, rows, axis):
-        n = count_of(axis)
-        here = j if axis == "gy" else i
-
-        def step(d, _):
-            arrival(src, dst, send, recv, rows, lax.rem(here + d, n), axis).wait_recv()
-            return 0
-
-        lax.fori_loop(1, n, step, 0)
+        for k in reversed(peers(axis)):
+            arrival(src, dst, send, recv, rows, k, axis).wait_recv()
 
     def sent_all(src, dst, send, recv, rows, axis):
-        n = count_of(axis)
-        here = j if axis == "gy" else i
-
-        def step(d, _):
-            arrival(src, dst, send, recv, rows, lax.rem(here + d, n), axis).wait_send()
-            return 0
-
-        lax.fori_loop(1, n, step, 0)
+        for k in peers(axis):
+            arrival(src, dst, send, recv, rows, k, axis).wait_send()
 
     coup_y = (csy, rcy, s_cy, r_cy, 8, "gy")
     coup_x = (csx, rcx, s_cx, r_cx, 8, "gx")
@@ -281,16 +268,16 @@
             sty[pl.ds(at + HALF + c, 8, stride=PACK), :] = tails[c]
 
     def wave(w):
-        def step(d, _):
-            k = lax.rem(j + d, 8) + 8 * w
-
-            @pl.when(k != j)
-            def _():
-                exchange(*tot_y[:5], k, "gy").start()
-
-            return 0
-
-        lax.fori_loop(0, 8, step, 0)
+        for b in (2, 1, 3, 0):
+            for a in range(2):
+                k = 8 * w + 4 * a + lax.rem(j + b, 4)
+                if b:
+                    exchange(*tot_y[:5], k, "gy").start()
+                else:
+
+                    @pl.when(k != j)
+                    def _():
+                        exchange(*tot_y[:5], k, "gy").start()
 
     z_and_y(0)
     z_and_y(2)
@@ -504,6 +491,7 @@
         for m in range(NI):
             extra(m, 0, jnext).start()
 
+    sent_all(*tot_x)
     recv_all(*ret_x)
     extra(0, 0, jnext).wait_recv()
     extra(0, 1, jprev).wait_recv()
@@ -537,6 +525,20 @@
 
     lax.fori_loop(0, X, x_finish, (tuple(rights), right_halo), unroll=4)
 
+    sent_all(*ret_x)
+
+    @pl.when(i == 0)
+    def _():
+        for m in range(NI):
+            extra(m, 1, jprev).wait_send()
+
+    @pl.when(i == NI - 1)
+    def _():
+        for m in range(NI):
+            extra(m, 0, jnext).wait_send()
+
+
+def advection(fb, c0, ax, bx, ayp, byp, azn, bzp, out_h, out, sem):
     def advect(x, _):
         rows = pl.ds(pl.multiple_of(x * Y, Y), Y)
         middle = c0[rows, :]
@@ -556,20 +558,15 @@
             out[c, rows, :] = result
         return 0
 
-    lax.fori_loop(0, X, advect, 0, unroll=8)
-
-    sent_all(*tot_x)
-    sent_all(*ret_x)
-
-    @pl.when(i == 0)
-    def _():
-        for m in range(NI):
-            extra(m, 1, jprev).wait_send()
-
-    @pl.when(i == NI - 1)
-    def _():
-        for m in range(NI):
-            extra(m, 0, jnext).wait_send()
+    stores = []
+    for part in range(4):
+        lax.fori_loop(part * 8, part * 8 + 8, advect, 0, unroll=8)
+        rows = pl.ds(part * 8 * Y, 8 * Y)
+        store = pltpu.make_async_copy(out.at[:, rows, :], out_h.at[:, rows, :], sem.at[part])
+        store.start()
+        stores.append(store)
+    for store in stores:
+        store.wait()
 
 
 def on_device(cotangent, diffusion, phase, courant, upwind):
@@ -587,21 +584,21 @@
         vm(NJ * PACK, Z), vm(NJ * PACK, Z), vm(NJ * PACK, Z), vm(NJ * PACK, Z),
         vm(NI * PACK, Z), vm(NI * PACK, Z), vm(NI * PACK, Z), vm(NI * PACK, Z), vm(2, 32, Z),
         vm(2, X, Z), vm(2, X, Z), vm(2, X, Z), vm(2, X, Z), vm(2, Y, Z), vm(2, Y, Z),
-        vm(LINES, Z), vm(LINES + 2 * Y, Z), vm(LINES + 2 * Y, Z), vm(X * PAD + 8, Z), vm(X * PAD + 8, Z), vm(LINES, Z), vm(LINES, Z),
-        vm(8 * PITCH, Z),
         dma((5,)),
         dma((NJ,)), dma((NJ,)), dma((NI,)), dma((NI,)), dma((2,)), dma((2,)), dma((2,)), dma((2,)), dma((2,)), dma((2,)),
         dma((NJ,)), dma((NJ,)), dma((NJ,)), dma((NJ,)), dma((NI,)), dma((NI,)), dma((NI,)), dma((NI,)),
         dma((2, NI)), dma((2,)),
     ]
-    out = pl.pallas_call(
+    vmem = pl.BlockSpec(memory_space=pltpu.VMEM)
+    shapes = [(8 * PITCH, Z), (LINES, Z), (LINES + 2 * Y, Z), (LINES + 2 * Y, Z), (X * PAD + 8, Z), (X * PAD + 8, Z), (LINES, Z), (LINES, Z)]
+    parts = pl.pallas_call(
         body,
-        out_shape=jax.ShapeDtypeStruct((C, LINES, Z), f32),
+        out_shape=[pltpu.VMEM(shape, f32) for shape in shapes],
         in_specs=[pl.BlockSpec(memory_space=pltpu.HBM)] * 5,
-        out_specs=pl.BlockSpec(memory_space=pltpu.VMEM),
+        out_specs=[vmem] * len(shapes),
         scratch_shapes=scratch,
         compiler_params=pltpu.CompilerParams(
-            collective_id=0, has_side_effects=True, vmem_limit_bytes=48 * 1024 * 1024
+            collective_id=0, has_side_effects=True, vmem_limit_bytes=40 * 1024 * 1024
         ),
     )(
         *(
@@ -615,6 +612,14 @@
             )
         )
     )
+    out = pl.pallas_call(
+        advection,
+        out_shape=jax.ShapeDtypeStruct((C, LINES, Z), f32),
+        in_specs=[vmem] * len(shapes),
+        out_specs=pl.BlockSpec(memory_space=pl.ANY),
+        scratch_shapes=[vm(C, LINES, Z), dma((4,))],
+        compiler_params=pltpu.CompilerParams(vmem_limit_bytes=8 * 1024 * 1024),
+    )(*(pltpu.with_memory_space_constraint(part, pltpu.VMEM) for part in parts))
     return out.reshape(C, X, Y, Z)
 
 

time: 35.3 us -> 33.8 us (0.958)
  local copies, waits for them, and re-layouts: 1.15 us -> 0 us
    unnamed x1 -> x0, local copies, waits for them, and re-layouts: 1.15 us -> none
    pallas_call x1 -> x2, Pallas kernels: 34 us -> 33.7 us  [the longest x1 32 us: on_device(): pl.pallas_call(body, out_shape=[pltpu.VMEM(shape, f32) for shape in shape...]
where the time goes in v3:
time: 33.8 us; the launch traced here: 33.7 us
  Pallas kernels  33.7 us (100%)
    pallas_call x1, Pallas kernels, on_device(): pl.pallas_call(body, out_shape=[pltpu.VMEM(shape, f32) for shape in shape...  32 us
    pallas_call x1, Pallas kernels, on_device(): pl.pallas_call(advection, out_shape=jax.ShapeDtypeStruct((C, LINES, Z), f...  1.68 us

profile of v3, /device:TPU:1, one launch (start us, length us, event | category | flops | bytes accessed | tf_op | source)
XLA Modules:
  0.0 33.7 jit_solution(14406981236314558790)
XLA Ops:
  0.0 32.0 %shard_map.55 = (f32[6592,128]{1,0:T(8,128)S(1)}, f32[512,128]{1,0:T(8,128)S(1)}, f32[544,128]{1,0:T(8,128)S(1)}, f32[544,128]{1,0:T(8,128)S(1)}, f32[776,128]{1...) custom-call(f32[6,512,128]{2,1,0:T(8,128)} %bitcast.6, ...), custom_call_target="tpu_custom_call" | custom-call | tf_op jit(solution)/shard_map/pallas_call | solution.py:594
  32.0 1.7 %shard_map.56 = f32[6,512,128]{2,1,0:T(8,128)} custom-call(f32[6592,128]{1,0:T(8,128)S(1)} %get-tuple-element.13.fb, f32[512,128]{1,0:T(8,128)S(1)} %get-tuple-element.14.c0, f32[544,128]{1,0:T(8,128)S(1)} %get-tuple-element.15.ax, f32[544,128]{1,0:T(8,128)S(1)} %get-tuple-element.16.bx, f32[776,128]{1,0:T(8,128)S(1)} %get-tuple-element.17.ayp, ...), custom_call_target="tpu_custom_call" | custom-call | tf_op jit(solution)/shard_map/pallas_call | solution.py:615

commit v4 on v3

--- a/solution.py
+++ b/solution.py
@@ -18,6 +18,7 @@
 PACK = 2 * HALF
 f32 = jnp.float32
 FAR = sorted(((a, b) for a in range(4) for b in range(4) if a or b), key=lambda d: -min(d[0], 4 - d[0]) - min(d[1], 4 - d[1]))
+ORDER = (0, 2, 1, 3)
 FAR_X = [(2, 1), (2, 0), (3, 1), (1, 1), (3, 0), (1, 0), (0, 1)]
 
 
@@ -38,8 +39,7 @@
     sty, tty, oty, rty, stx, ttx, otx, rtx, ext,
     fse, fre, fsy, fry, fsx, frx,
     in_sem,
-    s_cy, r_cy, s_cx, r_cx, s_fe, r_fe, s_fy, r_fy, s_fx, r_fx,
-    s_ty, r_ty, s_oy, r_oy, s_tx, r_tx, s_ox, r_ox, s_ex, r_ex,
+    sent, came,
 ):
     i = lax.axis_index("gx")
     j = lax.axis_index("gy")
@@ -49,12 +49,18 @@
     loads = [
         pltpu.make_async_copy(dif_h, dif, in_sem.at[0]),
         pltpu.make_async_copy(pha_h, pha, in_sem.at[1]),
-        pltpu.make_async_copy(cot_h, cot, in_sem.at[2]),
-        pltpu.make_async_copy(cou_h, cou, in_sem.at[3]),
-        pltpu.make_async_copy(upw_h, upw, in_sem.at[4]),
+        pltpu.make_async_copy(cou_h, cou, in_sem.at[2]),
+        pltpu.make_async_copy(upw_h, upw, in_sem.at[3]),
     ]
-    for load in loads[:3]:
-        load.start()
+    quarters = [pl.ds(q * 8 * Y, 8 * Y) for q in range(4)]
+    fields = [
+        pltpu.make_async_copy(cot_h.at[:, rows, :], cot.at[:, rows, :], in_sem.at[4 + q])
+        for q, rows in enumerate(quarters)
+    ]
+    loads[0].start()
+    loads[1].start()
+    for q in ORDER:
+        fields[q].start()
 
     barrier = pltpu.get_barrier_semaphore()
 
@@ -170,24 +176,25 @@
     outer = (i == 0) | (i == NI - 1)
     pl.semaphore_wait(barrier, NI + NJ - 2 + jnp.where(outer, NI - 1, 0))
 
-    def exchange(src, dst, send, recv, rows, k, axis):
+    def exchange(src, dst, slot, rows, k, axis):
         here = j if axis == "gy" else i
         return pltpu.make_async_remote_copy(
             src_ref=src.at[pl.ds(pl.multiple_of(k * rows, 8), rows), :],
             dst_ref=dst.at[pl.ds(pl.multiple_of(here * rows, 8), rows), :],
-            send_sem=send.at[k],
-            recv_sem=recv.at[here],
+            send_sem=sent.at[slot],
+            recv_sem=came.at[slot],
             device_id={axis: k},
             device_id_type=MESH,
         )
 
-    def arrival(src, dst, send, recv, rows, k, axis):
+    def whole_round(src, dst, slot, rows, axis):
+        total = pl.ds(0, rows * ((NJ if axis == "gy" else NI) - 1))
         return pltpu.make_async_remote_copy(
-            src_ref=src.at[pl.ds(pl.multiple_of(k * rows, 8), rows), :],
-            dst_ref=dst.at[pl.ds(pl.multiple_of(k * rows, 8), rows), :],
-            send_sem=send.at[k],
-            recv_sem=recv.at[k],
-            device_id={axis: k},
+            src_ref=src.at[total, :],
+            dst_ref=dst.at[total, :],
+            send_sem=sent.at[slot],
+            recv_sem=came.at[slot],
+            device_id={axis: jnext if axis == "gy" else inext},
             device_id_type=MESH,
         )
 
@@ -196,55 +203,58 @@
             return [lax.rem(j // 4 + a, 4) * 4 + lax.rem(j + b, 4) for a, b in FAR]
         return [lax.rem(i // 2 + a, 4) * 2 + lax.rem(i + b, 2) for a, b in FAR_X]
 
-    def send_all(src, dst, send, recv, rows, axis):
+    def send_all(src, dst, slot, rows, axis):
         here = j if axis == "gy" else i
         mine = pl.ds(pl.multiple_of(here * rows, 8), rows)
         for k in peers(axis):
-            exchange(src, dst, send, recv, rows, k, axis).start()
+            exchange(src, dst, slot, rows, k, axis).start()
         dst[mine, :] = src[mine, :]
 
-    def recv_all(src, dst, send, recv, rows, axis):
-        for k in reversed(peers(axis)):
-            arrival(src, dst, send, recv, rows, k, axis).wait_recv()
-
-    def sent_all(src, dst, send, recv, rows, axis):
-        for k in peers(axis):
-            arrival(src, dst, send, recv, rows, k, axis).wait_send()
-
-    coup_y = (csy, rcy, s_cy, r_cy, 8, "gy")
-    coup_x = (csx, rcx, s_cx, r_cx, 8, "gx")
-    tot_y = (sty, tty, s_ty, r_ty, PACK, "gy")
-    ret_y = (oty, rty, s_oy, r_oy, PACK, "gy")
-    tot_x = (stx, ttx, s_tx, r_tx, PACK, "gx")
-    ret_x = (otx, rtx, s_ox, r_ox, PACK, "gx")
-
-    def face(src, dst, send, recv, slot, axis, to):
+    def recv_all(src, dst, slot, rows, axis):
+        whole_round(src, dst, slot, rows, axis).wait_recv()
+
+    def sent_all(src, dst, slot, rows, axis):
+        whole_round(src, dst, slot, rows, axis).wait_send()
+
+    coup_y = (csy, rcy, 0, 8, "gy")
+    coup_x = (csx, rcx, 1, 8, "gx")
+    tot_y = (sty, tty, 2, PACK, "gy")
+    ret_y = (oty, rty, 3, PACK, "gy")
+    tot_x = (stx, ttx, 4, PACK, "gx")
+    ret_x = (otx, rtx, 5, PACK, "gx")
+
+    def face(src, dst, slot, part, axis, to):
         return pltpu.make_async_remote_copy(
-            src_ref=src.at[slot], dst_ref=dst.at[slot], send_sem=send.at[slot], recv_sem=recv.at[slot],
+            src_ref=src.at[part], dst_ref=dst.at[part], send_sem=sent.at[slot], recv_sem=came.at[slot],
             device_id={axis: to}, device_id_type=MESH,
         )
 
+    def both(src, dst, slot):
+        return pltpu.make_async_remote_copy(
+            src_ref=src, dst_ref=dst, send_sem=sent.at[slot], recv_sem=came.at[slot],
+            device_id={"gy": jnext}, device_id_type=MESH,
+        )
+
     edges = [
-        face(fse, fre, s_fe, r_fe, 0, "gy", jprev),
-        face(fse, fre, s_fe, r_fe, 1, "gy", jnext),
+        face(fse, fre, 6, 0, "gy", jprev),
+        face(fse, fre, 6, 1, "gy", jnext),
     ]
     faces = [
-        face(fsy, fry, s_fy, r_fy, 0, "gy", jprev),
-        face(fsy, fry, s_fy, r_fy, 1, "gy", jnext),
-        face(fsx, frx, s_fx, r_fx, 0, "gx", iprev),
-        face(fsx, frx, s_fx, r_fx, 1, "gx", inext),
+        face(fsy, fry, 7, 0, "gy", jprev),
+        face(fsy, fry, 7, 1, "gy", jnext),
+        face(fsx, frx, 8, 0, "gx", iprev),
+        face(fsx, frx, 8, 1, "gx", inext),
     ]
+    pairs = [both(fse, fre, 6), both(fsy, fry, 7), both(fsx, frx, 8)]
     send_all(*coup_y)
     fse[0] = ec[pl.ds(0, X, stride=Y), :]
     fse[1] = ec[pl.ds(Y - 1, X, stride=Y), :]
     for e in edges:
         e.start()
-    loads[2].wait()
-    loads[3].start()
-    loads[4].start()
 
     def z_and_y(q):
         rows = pl.ds(q * 8 * Y, 8 * Y)
+        fields[q].wait()
         scale, weight, finish = zt[rows, :], zw[rows, :], zo[rows, :]
         sums = [
             jnp.dot(split(cot[c, rows, :] * scale), tri[0], preferred_element_type=f32) for c in range(C)
@@ -272,15 +282,17 @@
             for a in range(2):
                 k = 8 * w + 4 * a + lax.rem(j + b, 4)
                 if b:
-                    exchange(*tot_y[:5], k, "gy").start()
+                    exchange(*tot_y[:4], k, "gy").start()
                 else:
 
                     @pl.when(k != j)
                     def _():
-                        exchange(*tot_y[:5], k, "gy").start()
+                        exchange(*tot_y[:4], k, "gy").start()
 
     z_and_y(0)
     z_and_y(2)
+    loads[2].start()
+    loads[3].start()
     wave(0)
     z_and_y(1)
     z_and_y(3)
@@ -318,8 +330,7 @@
         _, _, _, first = lax.fori_loop(0, X, down, (one, one, one, one), unroll=8)
         return first, rn
 
-    for e in edges:
-        e.wait_recv()
+    pairs[0].wait_recv()
     for x in range(X):
         xe[x, 0:Y, :] = ec[x * Y : (x + 1) * Y, :]
         xe[x, 16:24, :] = jnp.broadcast_to(fre[1, x : x + 1, :], (8, Z))
@@ -331,8 +342,8 @@
         csx[pl.ds(2 + r, 8, stride=8), :] = rn[r * 8 : r * 8 + 8]
         csx[pl.ds(4 + r, 8, stride=8), :] = last[r * 8 : r * 8 + 8]
 
+    loads[2].wait()
     loads[3].wait()
-    loads[4].wait()
     fsy[0] = upw[1, pl.ds(0, X, stride=Y), :].astype(f32) * cou[1, pl.ds(0, X, stride=Y), :]
     fsy[1] = (1.0 - upw[1, pl.ds(Y - 1, X, stride=Y), :].astype(f32)) * cou[1, pl.ds(Y - 1, X, stride=Y), :]
     fsx[0] = upw[0, 0:Y, :].astype(f32) * cou[0, 0:Y, :] * ec[0:Y, :]
@@ -390,8 +401,8 @@
 
     recv_all(*coup_x)
     reduce_factor(NI, rcx, kx)
-    for f in faces:
-        f.wait_recv()
+    pairs[1].wait_recv()
+    pairs[2].wait_recv()
 
     low_ok = jnp.where(j > 0, 1.0, 0.0).astype(f32)
     high_ok = jnp.where(j < NJ - 1, 1.0, 0.0).astype(f32)
@@ -422,7 +433,7 @@
 
     recv_all(*ret_y)
 
-    for q in (0, 2, 1, 3):
+    for q in ORDER:
         xs = pl.ds(q * 8, 8)
         at = (q % 2) * 8 * PACK + (q // 2) * C
         below, above, live = [], [], []
@@ -465,8 +476,8 @@
     sent_all(*coup_x)
     sent_all(*tot_y)
     sent_all(*ret_y)
-    for f in edges + faces:
-        f.wait_send()
+    for pair in pairs:
+        pair.wait_send()
     recv_all(*tot_x)
     reduce_solve(NI, ttx, kx, otx)
     send_all(*ret_x)
@@ -475,8 +486,8 @@
         return pltpu.make_async_remote_copy(
             src_ref=otx.at[pl.ds(pl.multiple_of(m * PACK, 8), PACK), :],
             dst_ref=ext.at[slot, pl.ds(0, PACK), :],
-            send_sem=s_ex.at[slot, m],
-            recv_sem=r_ex.at[slot],
+            send_sem=sent.at[9],
+            recv_sem=came.at[9],
             device_id=(m, to),
             device_id_type=MESH,
         )
@@ -493,8 +504,15 @@
 
     sent_all(*tot_x)
     recv_all(*ret_x)
-    extra(0, 0, jnext).wait_recv()
-    extra(0, 1, jprev).wait_recv()
+    extras = pltpu.make_async_remote_copy(
+        src_ref=otx,
+        dst_ref=rtx.at[pl.ds(0, 2 * PACK), :],
+        send_sem=sent.at[9],
+        recv_sem=came.at[9],
+        device_id={"gy": jnext},
+        device_id_type=MESH,
+    )
+    extras.wait_recv()
 
     lefts, rights = [], []
     for c in range(C):
@@ -527,15 +545,9 @@
 
     sent_all(*ret_x)
 
-    @pl.when(i == 0)
+    @pl.when(outer)
     def _():
-        for m in range(NI):
-            extra(m, 1, jprev).wait_send()
-
-    @pl.when(i == NI - 1)
-    def _():
-        for m in range(NI):
-            extra(m, 0, jnext).wait_send()
+        extras.wait_send()
 
 
 def advection(fb, c0, ax, bx, ayp, byp, azn, bzp, out_h, out, sem):
@@ -584,10 +596,7 @@
         vm(NJ * PACK, Z), vm(NJ * PACK, Z), vm(NJ * PACK, Z), vm(NJ * PACK, Z),
         vm(NI * PACK, Z), vm(NI * PACK, Z), vm(NI * PACK, Z), vm(NI * PACK, Z), vm(2, 32, Z),
         vm(2, X, Z), vm(2, X, Z), vm(2, X, Z), vm(2, X, Z), vm(2, Y, Z), vm(2, Y, Z),
-        dma((5,)),
-        dma((NJ,)), dma((NJ,)), dma((NI,)), dma((NI,)), dma((2,)), dma((2,)), dma((2,)), dma((2,)), dma((2,)), dma((2,)),
-        dma((NJ,)), dma((NJ,)), dma((NJ,)), dma((NJ,)), dma((NI,)), dma((NI,)), dma((NI,)), dma((NI,)),
-        dma((2, NI)), dma((2,)),
+        dma((8,)), dma((10,)), dma((10,)),
     ]
     vmem = pl.BlockSpec(memory_space=pltpu.VMEM)
     shapes = [(8 * PITCH, Z), (LINES, Z), (LINES + 2 * Y, Z), (LINES + 2 * Y, Z), (X * PAD + 8, Z), (X * PAD + 8, Z), (LINES, Z), (LINES, Z)]

time: 33.8 us -> 32.7 us (0.967)
  Pallas kernels: 33.7 us -> 32.6 us
    pallas_call x1, Pallas kernels: 32 us -> 30.9 us  [on_device(): pl.pallas_call(body, out_shape=[pltpu.VMEM(shape, f32) for shape in shape...]
where the time goes in v4:
time: 32.7 us; the launch traced here: 32.6 us
  Pallas kernels  32.6 us (100%)
    pallas_call x1, Pallas kernels, on_device(): pl.pallas_call(body, out_shape=[pltpu.VMEM(shape, f32) for shape in shape...  30.9 us
    pallas_call x1, Pallas kernels, on_device(): pl.pallas_call(advection, out_shape=jax.ShapeDtypeStruct((C, LINES, Z), f...  1.68 us

profile of v4, /device:TPU:1, one launch (start us, length us, event | category | flops | bytes accessed | tf_op | source)
XLA Modules:
  0.0 32.6 jit_solution(3018554090704377205)
XLA Ops:
  0.0 30.9 %shard_map.55 = (f32[6592,128]{1,0:T(8,128)S(1)}, f32[512,128]{1,0:T(8,128)S(1)}, f32[544,128]{1,0:T(8,128)S(1)}, f32[544,128]{1,0:T(8,128)S(1)}, f32[776,128]{1...) custom-call(f32[6,512,128]{2,1,0:T(8,128)} %bitcast.6, ...), custom_call_target="tpu_custom_call" | custom-call | tf_op jit(solution)/shard_map/pallas_call | solution.py:603
  30.9 1.7 %shard_map.56 = f32[6,512,128]{2,1,0:T(8,128)} custom-call(f32[6592,128]{1,0:T(8,128)S(1)} %get-tuple-element.13.fb, f32[512,128]{1,0:T(8,128)S(1)} %get-tuple-element.14.c0, f32[544,128]{1,0:T(8,128)S(1)} %get-tuple-element.15.ax, f32[544,128]{1,0:T(8,128)S(1)} %get-tuple-element.16.bx, f32[776,128]{1,0:T(8,128)S(1)} %get-tuple-element.17.ayp, ...), custom_call_target="tpu_custom_call" | custom-call | tf_op jit(solution)/shard_map/pallas_call | solution.py:624

commit v5 on v4

--- a/solution.py
+++ b/solution.py
@@ -16,6 +16,9 @@
 PITCH = PLANES * PAD + 8
 HALF = C * 2
 PACK = 2 * HALF
+HALF_X = HALF + 2
+PACK_X = 2 * HALF_X
+STEP_X = 32
 f32 = jnp.float32
 FAR = sorted(((a, b) for a in range(4) for b in range(4) if a or b), key=lambda d: -min(d[0], 4 - d[0]) - min(d[1], 4 - d[1]))
 ORDER = (0, 2, 1, 3)
@@ -74,14 +77,6 @@
 
     lax.fori_loop(1, NJ, greet_y, 0)
     lax.fori_loop(1, NI, greet_x, 0)
-
-    @pl.when(i != 0)
-    def _():
-        pl.semaphore_signal(barrier, inc=1, device_id=(0, jnext), device_id_type=MESH)
-
-    @pl.when(i != NI - 1)
-    def _():
-        pl.semaphore_signal(barrier, inc=1, device_id=(NI - 1, jprev), device_id_type=MESH)
 
     loads[0].wait()
     loads[1].wait()
@@ -173,21 +168,20 @@
     tri[0] = (row <= col).astype(f32).astype(jnp.bfloat16)
     tri[1] = (row >= col).astype(f32).astype(jnp.bfloat16)
 
-    outer = (i == 0) | (i == NI - 1)
-    pl.semaphore_wait(barrier, NI + NJ - 2 + jnp.where(outer, NI - 1, 0))
-
-    def exchange(src, dst, slot, rows, k, axis):
+    pl.semaphore_wait(barrier, NI + NJ - 2)
+
+    def exchange(src, dst, slot, pitch, rows, k, axis):
         here = j if axis == "gy" else i
         return pltpu.make_async_remote_copy(
-            src_ref=src.at[pl.ds(pl.multiple_of(k * rows, 8), rows), :],
-            dst_ref=dst.at[pl.ds(pl.multiple_of(here * rows, 8), rows), :],
+            src_ref=src.at[pl.ds(pl.multiple_of(k * pitch, 8), rows), :],
+            dst_ref=dst.at[pl.ds(pl.multiple_of(here * pitch, 8), rows), :],
             send_sem=sent.at[slot],
             recv_sem=came.at[slot],
             device_id={axis: k},
             device_id_type=MESH,
         )
 
-    def whole_round(src, dst, slot, rows, axis):
+    def whole_round(src, dst, slot, pitch, rows, axis):
         total = pl.ds(0, rows * ((NJ if axis == "gy" else NI) - 1))
         return pltpu.make_async_remote_copy(
             src_ref=src.at[total, :],
@@ -203,25 +197,25 @@
             return [lax.rem(j // 4 + a, 4) * 4 + lax.rem(j + b, 4) for a, b in FAR]
         return [lax.rem(i // 2 + a, 4) * 2 + lax.rem(i + b, 2) for a, b in FAR_X]
 
-    def send_all(src, dst, slot, rows, axis):
+    def send_all(src, dst, slot, pitch, rows, axis):
         here = j if axis == "gy" else i
-        mine = pl.ds(pl.multiple_of(here * rows, 8), rows)
+        mine = pl.ds(pl.multiple_of(here * pitch, 8), rows)
         for k in peers(axis):
-            exchange(src, dst, slot, rows, k, axis).start()
+            exchange(src, dst, slot, pitch, rows, k, axis).start()
         dst[mine, :] = src[mine, :]
 
-    def recv_all(src, dst, slot, rows, axis):
-        whole_round(src, dst, slot, rows, axis).wait_recv()
-
-    def sent_all(src, dst, slot, rows, axis):
-        whole_round(src, dst, slot, rows, axis).wait_send()
-
-    coup_y = (csy, rcy, 0, 8, "gy")
-    coup_x = (csx, rcx, 1, 8, "gx")
-    tot_y = (sty, tty, 2, PACK, "gy")
-    ret_y = (oty, rty, 3, PACK, "gy")
-    tot_x = (stx, ttx, 4, PACK, "gx")
-    ret_x = (otx, rtx, 5, PACK, "gx")
+    def recv_all(src, dst, slot, pitch, rows, axis):
+        whole_round(src, dst, slot, pitch, rows, axis).wait_recv()
+
+    def sent_all(src, dst, slot, pitch, rows, axis):
+        whole_round(src, dst, slot, pitch, rows, axis).wait_send()
+
+    coup_y = (csy, rcy, 0, 8, 8, "gy")
+    coup_x = (csx, rcx, 1, 16, 16, "gx")
+    tot_y = (sty, tty, 2, PACK, PACK, "gy")
+    ret_y = (oty, rty, 3, PACK, PACK, "gy")
+    tot_x = (stx, ttx, 4, STEP_X, PACK_X, "gx")
+    ret_x = (otx, rtx, 5, STEP_X, PACK_X, "gx")
 
     def face(src, dst, slot, part, axis, to):
         return pltpu.make_async_remote_copy(
@@ -282,12 +276,12 @@
             for a in range(2):
                 k = 8 * w + 4 * a + lax.rem(j + b, 4)
                 if b:
-                    exchange(*tot_y[:4], k, "gy").start()
+                    exchange(*tot_y[:5], k, "gy").start()
                 else:
 
                     @pl.when(k != j)
                     def _():
-                        exchange(*tot_y[:4], k, "gy").start()
+                        exchange(*tot_y[:5], k, "gy").start()
 
     z_and_y(0)
     z_and_y(2)
@@ -336,11 +330,12 @@
         xe[x, 16:24, :] = jnp.broadcast_to(fre[1, x : x + 1, :], (8, Z))
         xe[x, 24:32, :] = jnp.broadcast_to(fre[0, x : x + 1, :], (8, Z))
     first, rn = x_factor()
-    last = xb[X - 1, 0:Y, :]
-    for r in range(2):
-        csx[pl.ds(r, 8, stride=8), :] = first[r * 8 : r * 8 + 8]
-        csx[pl.ds(2 + r, 8, stride=8), :] = rn[r * 8 : r * 8 + 8]
-        csx[pl.ds(4 + r, 8, stride=8), :] = last[r * 8 : r * 8 + 8]
+    for t, part in enumerate((first, rn, xb[X - 1])):
+        for r in range(2):
+            csx[pl.ds(4 * t + r, 8, stride=16), :] = part[r * 8 : r * 8 + 8]
+        csx[pl.ds(4 * t + 2, C, stride=16), :] = part[16 : 16 + C]
+        csx[pl.ds(C * 16 + 4 * t + 2, 8 - C, stride=16), :] = part[24 : 32 - C]
+        csx[pl.ds(4 * t + 3, 8, stride=16), :] = part[24:32]
 
     loads[2].wait()
     loads[3].wait()
@@ -353,54 +348,52 @@
     for f in faces:
         f.start()
 
-    def reduce_factor(count, couplings, factors):
-        def pair(base, t):
+    def reduce_factor(count, pitch, lines, half, couplings, factors):
+        def spread(base, t):
+            at = base + len(lines) * t
             return jnp.concatenate(
-                [
-                    jnp.broadcast_to(couplings[pl.ds(base + 2 * t, 1), :], (C, Z)),
-                    jnp.broadcast_to(couplings[pl.ds(base + 2 * t + 1, 1), :], (C, Z)),
-                ],
+                [jnp.broadcast_to(couplings[pl.ds(at + n, 1), :], (wide, Z)) for n, wide in enumerate(lines)],
                 axis=0,
             )
 
-        edge = jnp.zeros((HALF, Z), f32)
+        edge = jnp.zeros((half, Z), f32)
         for m in range(count):
-            a1, b1, bn = pair(m * 8, 0), pair(m * 8, 1), pair(m * 8, 2)
+            a1, b1, bn = spread(m * pitch, 0), spread(m * pitch, 1), spread(m * pitch, 2)
             alpha = 1.0 / (1.0 - a1 * edge)
             alpha_a = a1 * alpha
             forward = b1 * alpha
             back = b1 * edge
-            factors[0, m, 0:HALF, :] = alpha
-            factors[1, m, 0:HALF, :] = alpha_a
-            factors[2, m, 0:HALF, :] = forward
-            factors[3, m, 0:HALF, :] = edge
-            factors[4, m, 0:HALF, :] = back * alpha
-            factors[5, m, 0:HALF, :] = b1 + back * alpha_a
+            factors[0, m, 0:half, :] = alpha
+            factors[1, m, 0:half, :] = alpha_a
+            factors[2, m, 0:half, :] = forward
+            factors[3, m, 0:half, :] = edge
+            factors[4, m, 0:half, :] = back * alpha
+            factors[5, m, 0:half, :] = b1 + back * alpha_a
             edge = bn + back * forward
 
-    def reduce_solve(count, totals, factors, results):
-        gain = jnp.zeros((HALF, Z), f32)
+    def reduce_solve(count, pitch, half, totals, factors, results):
+        gain = jnp.zeros((half, Z), f32)
         for m in range(count):
-            head = totals[m * PACK : m * PACK + HALF, :]
-            tail = totals[m * PACK + HALF : m * PACK + PACK, :]
-            gl[0, m, 0:HALF, :] = gain
-            gl[1, m, 0:HALF, :] = factors[0, m, 0:HALF, :] * head + factors[1, m, 0:HALF, :] * gain
-            gain = tail + factors[4, m, 0:HALF, :] * head + factors[5, m, 0:HALF, :] * gain
-        later = jnp.zeros((HALF, Z), f32)
+            head = totals[m * pitch : m * pitch + half, :]
+            tail = totals[m * pitch + half : m * pitch + 2 * half, :]
+            gl[0, m, 0:half, :] = gain
+            gl[1, m, 0:half, :] = factors[0, m, 0:half, :] * head + factors[1, m, 0:half, :] * gain
+            gain = tail + factors[4, m, 0:half, :] * head + factors[5, m, 0:half, :] * gain
+        later = jnp.zeros((half, Z), f32)
         for m in range(count - 1, -1, -1):
-            results[m * PACK + HALF : m * PACK + PACK, :] = later
-            later = gl[1, m, 0:HALF, :] + factors[2, m, 0:HALF, :] * later
-            results[m * PACK : m * PACK + HALF, :] = gl[0, m, 0:HALF, :] + factors[3, m, 0:HALF, :] * later
+            results[m * pitch + half : m * pitch + 2 * half, :] = later
+            later = gl[1, m, 0:half, :] + factors[2, m, 0:half, :] * later
+            results[m * pitch : m * pitch + half, :] = gl[0, m, 0:half, :] + factors[3, m, 0:half, :] * later
 
     recv_all(*coup_y)
-    reduce_factor(NJ, rcy, ky)
+    reduce_factor(NJ, 8, (C, C), HALF, rcy, ky)
 
     recv_all(*tot_y)
-    reduce_solve(NJ, tty, ky, oty)
+    reduce_solve(NJ, PACK, HALF, tty, ky, oty)
     send_all(*ret_y)
 
     recv_all(*coup_x)
-    reduce_factor(NI, rcx, kx)
+    reduce_factor(NI, 16, (C, C, 1, 1), HALF_X, rcx, kx)
     pairs[1].wait_recv()
     pairs[2].wait_recv()
 
@@ -451,7 +444,7 @@
                 ay[c, pl.ds(q * 8 * Y + y, 8, stride=Y), :] = live[c] * finish
 
     def x_totals(x, carry):
-        heads, tails, halo = carry
+        heads, tails, halo_head, halo = carry
         rows = pl.ds(pl.multiple_of(x * Y, Y), Y)
         a, b = xa[x, 0:Y, :], xb[x, 0:Y, :]
         new_heads, new_tails = [], []
@@ -461,16 +454,23 @@
             tail = tails[c] + b * value
             new_tails.append(tail)
             ay[c, rows, :] = tail
-        halo = halo + xb[x, 16:32, :] * ayh[rows, :]
+        value = ayh[rows, :]
+        halo_head = halo_head + xa[x, 16:32, :] * value
+        halo = halo + xb[x, 16:32, :] * value
         ayh[rows, :] = halo
-        return tuple(new_heads), tuple(new_tails), halo
+        return tuple(new_heads), tuple(new_tails), halo_head, halo
 
     none = jnp.zeros((Y, Z), f32)
-    heads, tails, _ = lax.fori_loop(0, X, x_totals, ((none,) * C, (none,) * C, none), unroll=8)
+    heads, tails, *edge_pair = lax.fori_loop(0, X, x_totals, ((none,) * C, (none,) * C, none, none), unroll=8)
     for c in range(C):
         for r in range(2):
-            stx[pl.ds(r * C + c, 8, stride=PACK), :] = heads[c][r * 8 : r * 8 + 8]
-            stx[pl.ds(HALF + r * C + c, 8, stride=PACK), :] = tails[c][r * 8 : r * 8 + 8]
+            stx[pl.ds(r * C + c, 8, stride=STEP_X), :] = heads[c][r * 8 : r * 8 + 8]
+            stx[pl.ds(HALF_X + r * C + c, 8, stride=STEP_X), :] = tails[c][r * 8 : r * 8 + 8]
+    for end, part in enumerate(edge_pair):
+        at = end * HALF_X + HALF
+        stx[pl.ds(at, C, stride=STEP_X), :] = part[0:C]
+        stx[pl.ds(C * STEP_X + at, 8 - C, stride=STEP_X), :] = part[8 : 16 - C]
+        stx[pl.ds(at + 1, 2 * C - 8, stride=STEP_X), :] = part[16 - C : 8 + C]
     send_all(*tot_x)
     sent_all(*coup_y)
     sent_all(*coup_x)
@@ -479,51 +479,27 @@
     for pair in pairs:
         pair.wait_send()
     recv_all(*tot_x)
-    reduce_solve(NI, ttx, kx, otx)
+    reduce_solve(NI, STEP_X, HALF_X, ttx, kx, otx)
     send_all(*ret_x)
-
-    def extra(m, slot, to):
-        return pltpu.make_async_remote_copy(
-            src_ref=otx.at[pl.ds(pl.multiple_of(m * PACK, 8), PACK), :],
-            dst_ref=ext.at[slot, pl.ds(0, PACK), :],
-            send_sem=sent.at[9],
-            recv_sem=came.at[9],
-            device_id=(m, to),
-            device_id_type=MESH,
-        )
-
-    @pl.when(i == 0)
-    def _():
-        for m in range(NI):
-            extra(m, 1, jprev).start()
-
-    @pl.when(i == NI - 1)
-    def _():
-        for m in range(NI):
-            extra(m, 0, jnext).start()
 
     sent_all(*tot_x)
     recv_all(*ret_x)
-    extras = pltpu.make_async_remote_copy(
-        src_ref=otx,
-        dst_ref=rtx.at[pl.ds(0, 2 * PACK), :],
-        send_sem=sent.at[9],
-        recv_sem=came.at[9],
-        device_id={"gy": jnext},
-        device_id_type=MESH,
-    )
-    extras.wait_recv()
 
     lefts, rights = [], []
     for c in range(C):
-        left = jnp.concatenate([rtx[pl.ds(r * C + c, 8, stride=PACK), :] for r in range(2)], axis=0)
-        right = jnp.concatenate([rtx[pl.ds(HALF + r * C + c, 8, stride=PACK), :] for r in range(2)], axis=0)
+        left = jnp.concatenate([rtx[pl.ds(r * C + c, 8, stride=STEP_X), :] for r in range(2)], axis=0)
+        right = jnp.concatenate([rtx[pl.ds(HALF_X + r * C + c, 8, stride=STEP_X), :] for r in range(2)], axis=0)
         fb[pl.ds(c * PITCH + 8, Y), :] = left
         fb[pl.ds(c * PITCH + (X + 1) * PAD + 8, Y), :] = right
         lefts.append(left * xr[0:Y, :])
         rights.append(right)
-    left_halo = jnp.concatenate([ext[0, 6:14, :], ext[1, 0:8, :]], axis=0) * xr[16:32, :]
-    right_halo = jnp.concatenate([ext[0, 18:26, :], ext[1, 12:20, :]], axis=0)
+    for end in range(2):
+        at = end * HALF_X + HALF
+        ext[end, 0:C, :] = rtx[pl.ds(at, C, stride=STEP_X), :]
+        ext[end, 8 : 16 - C, :] = rtx[pl.ds(C * STEP_X + at, 8 - C, stride=STEP_X), :]
+        ext[end, 16 - C : 8 + C, :] = rtx[pl.ds(at + 1, 2 * C - 8, stride=STEP_X), :]
+    left_halo = ext[0] * xr[16:32, :]
+    right_halo = ext[1]
 
     def x_finish(step, carry):
         x = X - 1 - step
@@ -544,10 +520,6 @@
     lax.fori_loop(0, X, x_finish, (tuple(rights), right_halo), unroll=4)
 
     sent_all(*ret_x)
-
-    @pl.when(outer)
-    def _():
-        extras.wait_send()
 
 
 def advection(fb, c0, ax, bx, ayp, byp, azn, bzp, out_h, out, sem):
@@ -592,11 +564,11 @@
         vm(LINES // Z, Z, Z), vm(LINES, Z), vm(LINES, Z), vm(LINES, Z), vm(C, LINES, Z), vm(2, 2 * Z, Z, dtype=jnp.bfloat16),
         vm(Y, X, Z), vm(Y, X, Z), vm(Y, X, Z), vm(Y, X, Z), vm(X, Z), vm(C, Y, X, Z), vm(C, LINES, Z), vm(X * 16, Z),
         vm(X, 32, Z), vm(X, 32, Z), vm(X, 32, Z), vm(X, 32, Z), vm(X, 32, Z), vm(32, Z),
-        vm(NJ * 8, Z), vm(NI * 8, Z), vm(NJ * 8, Z), vm(NI * 8, Z), vm(6, NJ, 16, Z), vm(6, NI, 16, Z), vm(2, NJ, 16, Z),
+        vm(NJ * 8, Z), vm(NI * 16, Z), vm(NJ * 8, Z), vm(NI * 16, Z), vm(6, NJ, 16, Z), vm(6, NI, 16, Z), vm(2, NJ, 16, Z),
         vm(NJ * PACK, Z), vm(NJ * PACK, Z), vm(NJ * PACK, Z), vm(NJ * PACK, Z),
-        vm(NI * PACK, Z), vm(NI * PACK, Z), vm(NI * PACK, Z), vm(NI * PACK, Z), vm(2, 32, Z),
+        vm(NI * STEP_X, Z), vm(NI * STEP_X, Z), vm(NI * STEP_X, Z), vm(NI * STEP_X, Z), vm(2, 16, Z),
         vm(2, X, Z), vm(2, X, Z), vm(2, X, Z), vm(2, X, Z), vm(2, Y, Z), vm(2, Y, Z),
-        dma((8,)), dma((10,)), dma((10,)),
+        dma((8,)), dma((9,)), dma((9,)),
     ]
     vmem = pl.BlockSpec(memory_space=pltpu.VMEM)
     shapes = [(8 * PITCH, Z), (LINES, Z), (LINES + 2 * Y, Z), (LINES + 2 * Y, Z), (X * PAD + 8, Z), (X * PAD + 8, Z), (LINES, Z), (LINES, Z)]

time: 32.7 us -> 31.7 us (0.969)
  Pallas kernels: 32.6 us -> 31.6 us
    pallas_call x1, Pallas kernels: 30.9 us -> 29.9 us  [on_device(): pl.pallas_call(body, out_shape=[pltpu.VMEM(shape, f32) for shape in shape...]
where the time goes in v5:
time: 31.7 us; the launch traced here: 31.6 us
  Pallas kernels  31.6 us (100%)
    pallas_call x1, Pallas kernels, on_device(): pl.pallas_call(body, out_shape=[pltpu.VMEM(shape, f32) for shape in shape...  29.9 us
    pallas_call x1, Pallas kernels, on_device(): pl.pallas_call(advection, out_shape=jax.ShapeDtypeStruct((C, LINES, Z), f...  1.68 us

profile of v5, /device:TPU:1, one launch (start us, length us, event | category | flops | bytes accessed | tf_op | source)
XLA Modules:
  0.0 31.6 jit_solution(17641354562995057435)
XLA Ops:
  0.0 29.9 %shard_map.55 = (f32[6592,128]{1,0:T(8,128)S(1)}, f32[512,128]{1,0:T(8,128)S(1)}, f32[544,128]{1,0:T(8,128)S(1)}, f32[544,128]{1,0:T(8,128)S(1)}, f32[776,128]{1...) custom-call(f32[6,512,128]{2,1,0:T(8,128)} %bitcast.6, ...), custom_call_target="tpu_custom_call" | custom-call | tf_op jit(solution)/shard_map/pallas_call | solution.py:575
  29.9 1.7 %shard_map.56 = f32[6,512,128]{2,1,0:T(8,128)} custom-call(f32[6592,128]{1,0:T(8,128)S(1)} %get-tuple-element.13.fb, f32[512,128]{1,0:T(8,128)S(1)} %get-tuple-element.14.c0, f32[544,128]{1,0:T(8,128)S(1)} %get-tuple-element.15.ax, f32[544,128]{1,0:T(8,128)S(1)} %get-tuple-element.16.bx, f32[776,128]{1,0:T(8,128)S(1)} %get-tuple-element.17.ayp, ...), custom_call_target="tpu_custom_call" | custom-call | tf_op jit(solution)/shard_map/pallas_call | solution.py:596

commit v6 on v5

--- a/solution.py
+++ b/solution.py
@@ -168,8 +168,6 @@
     tri[0] = (row <= col).astype(f32).astype(jnp.bfloat16)
     tri[1] = (row >= col).astype(f32).astype(jnp.bfloat16)
 
-    pl.semaphore_wait(barrier, NI + NJ - 2)
-
     def exchange(src, dst, slot, pitch, rows, k, axis):
         here = j if axis == "gy" else i
         return pltpu.make_async_remote_copy(
@@ -240,22 +238,21 @@
         face(fsx, frx, 8, 1, "gx", inext),
     ]
     pairs = [both(fse, fre, 6), both(fsy, fry, 7), both(fsx, frx, 8)]
-    send_all(*coup_y)
-    fse[0] = ec[pl.ds(0, X, stride=Y), :]
-    fse[1] = ec[pl.ds(Y - 1, X, stride=Y), :]
-    for e in edges:
-        e.start()
-
-    def z_and_y(q):
-        rows = pl.ds(q * 8 * Y, 8 * Y)
-        fields[q].wait()
-        scale, weight, finish = zt[rows, :], zw[rows, :], zo[rows, :]
-        sums = [
-            jnp.dot(split(cot[c, rows, :] * scale), tri[0], preferred_element_type=f32) for c in range(C)
-        ]
+    def z_lower(q):
+        rows = quarters[q]
+        scale, weight = zt[rows, :], zw[rows, :]
         for c in range(C):
-            whole = jnp.dot(split(sums[c] * weight), tri[1], preferred_element_type=f32)
-            zb[c, rows, :] = whole * finish
+            zb[c, rows, :] = weight * jnp.dot(
+                split(cot[c, rows, :] * scale), tri[0], preferred_element_type=f32
+            )
+
+    def z_upper(q):
+        rows = quarters[q]
+        finish = zo[rows, :]
+        for c in range(C):
+            zb[c, rows, :] = finish * jnp.dot(split(zb[c, rows, :]), tri[1], preferred_element_type=f32)
+
+    def y_totals(q):
         xs = pl.ds(q * 8, 8)
         heads = [jnp.zeros((8, Z), f32) for _ in range(C)]
         tails = [jnp.zeros((8, Z), f32) for _ in range(C)]
@@ -271,28 +268,24 @@
             sty[pl.ds(at + c, 8, stride=PACK), :] = heads[c]
             sty[pl.ds(at + HALF + c, 8, stride=PACK), :] = tails[c]
 
-    def wave(w):
-        for b in (2, 1, 3, 0):
-            for a in range(2):
-                k = 8 * w + 4 * a + lax.rem(j + b, 4)
-                if b:
-                    exchange(*tot_y[:5], k, "gy").start()
-                else:
-
-                    @pl.when(k != j)
-                    def _():
-                        exchange(*tot_y[:5], k, "gy").start()
-
-    z_and_y(0)
-    z_and_y(2)
+    for q in ORDER:
+        fields[q].wait()
     loads[2].start()
     loads[3].start()
-    wave(0)
-    z_and_y(1)
-    z_and_y(3)
-    wave(1)
-    mine_y = pl.ds(pl.multiple_of(j * PACK, 8), PACK)
-    tty[mine_y, :] = sty[mine_y, :]
+    z_lower(0)
+    for q in range(4):
+        if q < 3:
+            z_lower(q + 1)
+        z_upper(q)
+        y_totals(q)
+
+    pl.semaphore_wait(barrier, NI + NJ - 2)
+    send_all(*tot_y)
+    send_all(*coup_y)
+    fse[0] = ec[pl.ds(0, X, stride=Y), :]
+    fse[1] = ec[pl.ds(Y - 1, X, stride=Y), :]
+    for e in edges:
+        e.start()
 
     def x_factor():
         rows = pl.ds(0, 32)

time: 31.7 us -> 31.4 us (level)
  no operation moved by 1% of the time
where the time goes in v6:
time: 31.4 us; the launch traced here: 31.3 us
  Pallas kernels  31.3 us (100%)
    pallas_call x1, Pallas kernels, on_device(): pl.pallas_call(body, out_shape=[pltpu.VMEM(shape, f32) for shape in shape...  29.6 us
    pallas_call x1, Pallas kernels, on_device(): pl.pallas_call(advection, out_shape=jax.ShapeDtypeStruct((C, LINES, Z), f...  1.68 us

profile of v6, /device:TPU:1, one launch (start us, length us, event | category | flops | bytes accessed | tf_op | source)
XLA Modules:
  0.0 31.3 jit_solution(6751764418278401855)
XLA Ops:
  0.0 29.6 %shard_map.55 = (f32[6592,128]{1,0:T(8,128)S(1)}, f32[512,128]{1,0:T(8,128)S(1)}, f32[544,128]{1,0:T(8,128)S(1)}, f32[544,128]{1,0:T(8,128)S(1)}, f32[776,128]{1...) custom-call(f32[6,512,128]{2,1,0:T(8,128)} %bitcast.6, ...), custom_call_target="tpu_custom_call" | custom-call | tf_op jit(solution)/shard_map/pallas_call | solution.py:568
  29.6 1.7 %shard_map.56 = f32[6,512,128]{2,1,0:T(8,128)} custom-call(f32[6592,128]{1,0:T(8,128)S(1)} %get-tuple-element.13.fb, f32[512,128]{1,0:T(8,128)S(1)} %get-tuple-element.14.c0, f32[544,128]{1,0:T(8,128)S(1)} %get-tuple-element.15.ax, f32[544,128]{1,0:T(8,128)S(1)} %get-tuple-element.16.bx, f32[776,128]{1,0:T(8,128)S(1)} %get-tuple-element.17.ayp, ...), custom_call_target="tpu_custom_call" | custom-call | tf_op jit(solution)/shard_map/pallas_call | solution.py:589

commit v7 on v6

--- a/solution.py
+++ b/solution.py
@@ -36,7 +36,7 @@
     fb, c0, ax, bx, ayp, byp, azn, bzp,
     cot, dif, pha, cou, upw, ec,
     et, zt, zw, zo, zb, tri,
-    yb, ya, yw, yo, yr, yf, ay, ayh,
+    yb, ya, yw, yo, yr, yf, ay, ayh, ynl, ynr, ends,
     xe, xb, xa, xw, xo, xr,
     csy, csx, rcy, rcx, ky, kx, gl,
     sty, tty, oty, rty, stx, ttx, otx, rtx, ext,
@@ -417,44 +417,73 @@
     ayp[pl.ds(PAD, X, stride=PAD), :] = fry[0] * high_ok
     ayh[...] = jnp.zeros_like(ayh)
 
+    for q in range(4):
+        xs = pl.ds(q * 8, 8)
+        live = [jnp.zeros((8, Z), f32) for _ in range(C)]
+        summed = jnp.zeros((8, Z), f32)
+        for y in range(Y - 1, -1, -1):
+            cells = pl.ds(q * 8 * Y + y, 8, stride=Y)
+            weight, finish = yw[y, xs, :], yo[y, xs, :]
+            summed = summed + weight
+            ynl[cells, :] = finish * (summed * yr[xs, :])
+            ynr[cells, :] = finish
+            for c in range(C):
+                live[c] = live[c] + weight * yf[c, y, xs, :]
+                ay[c, cells, :] = live[c] * finish
+
+    def x_totals(x, carry):
+        heads, tails = carry
+        rows = pl.ds(pl.multiple_of(x * Y, Y), Y)
+        a, b = xa[x, 0:Y, :], xb[x, 0:Y, :]
+        left, right = ynl[rows, :], ynr[rows, :]
+        ends[0, rows, :] = a * left
+        ends[1, rows, :] = a * right
+        ends[2, rows, :] = b * left
+        ends[3, rows, :] = b * right
+        values = [ay[c, rows, :] for c in range(C)]
+        return (
+            tuple(heads[c] + a * values[c] for c in range(C)),
+            tuple(tails[c] + b * values[c] for c in range(C)),
+        )
+
+    none = jnp.zeros((Y, Z), f32)
+    heads, tails = lax.fori_loop(0, X, x_totals, ((none,) * C, (none,) * C), unroll=8)
+    heads, tails = list(heads), list(tails)
+
     recv_all(*ret_y)
 
-    for q in ORDER:
+    def end_values(x, c):
+        at = lax.rem(x, NJ) * PACK + (x // NJ) * C + c
+        return (
+            jnp.broadcast_to(rty[pl.ds(at, 1), :], (Y, Z)),
+            jnp.broadcast_to(rty[pl.ds(at + HALF, 1), :], (Y, Z)),
+        )
+
+    for q in range(4):
         xs = pl.ds(q * 8, 8)
         at = (q % 2) * 8 * PACK + (q // 2) * C
-        below, above, live = [], [], []
         for c in range(C):
             left = rty[pl.ds(at + c, 8, stride=PACK), :]
             right = rty[pl.ds(at + HALF + c, 8, stride=PACK), :]
             ayh[pl.ds(q * 8 * 16 + c, 8, stride=16), :] = left * fre[1, xs, :]
             ayh[pl.ds(q * 8 * 16 + 8 + c, 8, stride=16), :] = right * fre[0, xs, :]
-            below.append(left * yr[xs, :])
-            live.append(right)
-        for y in range(Y - 1, -1, -1):
-            weight, finish = yw[y, xs, :], yo[y, xs, :]
-            for c in range(C):
-                live[c] = live[c] + weight * (yf[c, y, xs, :] + below[c])
-                ay[c, pl.ds(q * 8 * Y + y, 8, stride=Y), :] = live[c] * finish
-
-    def x_totals(x, carry):
-        heads, tails, halo_head, halo = carry
+
+    def end_totals(x, carry):
+        heads, tails, halo_head, halo_tail = carry
         rows = pl.ds(pl.multiple_of(x * Y, Y), Y)
-        a, b = xa[x, 0:Y, :], xb[x, 0:Y, :]
-        new_heads, new_tails = [], []
-        for c in range(C):
-            value = ay[c, rows, :]
-            new_heads.append(heads[c] + a * value)
-            tail = tails[c] + b * value
-            new_tails.append(tail)
-            ay[c, rows, :] = tail
+        hl, hr, tl, tr = (ends[n, rows, :] for n in range(4))
+        pairs_of = [end_values(x, c) for c in range(C)]
         value = ayh[rows, :]
-        halo_head = halo_head + xa[x, 16:32, :] * value
-        halo = halo + xb[x, 16:32, :] * value
-        ayh[rows, :] = halo
-        return tuple(new_heads), tuple(new_tails), halo_head, halo
-
-    none = jnp.zeros((Y, Z), f32)
-    heads, tails, *edge_pair = lax.fori_loop(0, X, x_totals, ((none,) * C, (none,) * C, none, none), unroll=8)
+        return (
+            tuple(heads[c] + (hl * left + hr * right) for c, (left, right) in enumerate(pairs_of)),
+            tuple(tails[c] + (tl * left + tr * right) for c, (left, right) in enumerate(pairs_of)),
+            halo_head + xa[x, 16:32, :] * value,
+            halo_tail + xb[x, 16:32, :] * value,
+        )
+
+    heads, tails, *edge_pair = lax.fori_loop(
+        0, X, end_totals, (tuple(heads), tuple(tails), none, none), unroll=8
+    )
     for c in range(C):
         for r in range(2):
             stx[pl.ds(r * C + c, 8, stride=STEP_X), :] = heads[c][r * 8 : r * 8 + 8]
@@ -465,6 +494,23 @@
         stx[pl.ds(C * STEP_X + at, 8 - C, stride=STEP_X), :] = part[8 : 16 - C]
         stx[pl.ds(at + 1, 2 * C - 8, stride=STEP_X), :] = part[16 - C : 8 + C]
     send_all(*tot_x)
+
+    def x_prefix(x, carry):
+        tails, halo = carry
+        rows = pl.ds(pl.multiple_of(x * Y, Y), Y)
+        b = xb[x, 0:Y, :]
+        by_left, by_right = ynl[rows, :], ynr[rows, :]
+        out = []
+        for c in range(C):
+            left, right = end_values(x, c)
+            tail = tails[c] + b * (ay[c, rows, :] + by_left * left + by_right * right)
+            ay[c, rows, :] = tail
+            out.append(tail)
+        halo = halo + xb[x, 16:32, :] * ayh[rows, :]
+        ayh[rows, :] = halo
+        return tuple(out), halo
+
+    lax.fori_loop(0, X, x_prefix, ((none,) * C, none), unroll=8)
     sent_all(*coup_y)
     sent_all(*coup_x)
     sent_all(*tot_y)
@@ -555,7 +601,7 @@
         vm(C, LINES, Z), vm(LINES, Z), vm(LINES, Z, dtype=jnp.int32), vm(3, LINES, Z), vm(3, LINES, Z, dtype=jnp.int32),
         vm(LINES, Z),
         vm(LINES // Z, Z, Z), vm(LINES, Z), vm(LINES, Z), vm(LINES, Z), vm(C, LINES, Z), vm(2, 2 * Z, Z, dtype=jnp.bfloat16),
-        vm(Y, X, Z), vm(Y, X, Z), vm(Y, X, Z), vm(Y, X, Z), vm(X, Z), vm(C, Y, X, Z), vm(C, LINES, Z), vm(X * 16, Z),
+        vm(Y, X, Z), vm(Y, X, Z), vm(Y, X, Z), vm(Y, X, Z), vm(X, Z), vm(C, Y, X, Z), vm(C, LINES, Z), vm(X * 16, Z), vm(LINES, Z), vm(LINES, Z), vm(4, LINES, Z),
         vm(X, 32, Z), vm(X, 32, Z), vm(X, 32, Z), vm(X, 32, Z), vm(X, 32, Z), vm(32, Z),
         vm(NJ * 8, Z), vm(NI * 16, Z), vm(NJ * 8, Z), vm(NI * 16, Z), vm(6, NJ, 16, Z), vm(6, NI, 16, Z), vm(2, NJ, 16, Z),
         vm(NJ * PACK, Z), vm(NJ * PACK, Z), vm(NJ * PACK, Z), vm(NJ * PACK, Z),

time: 31.4 us -> 32.1 us (1.022)
  Pallas kernels: 31.3 us -> 31.9 us
    pallas_call x1, Pallas kernels: 29.6 us -> 30.3 us  [on_device(): pl.pallas_call(body, out_shape=[pltpu.VMEM(shape, f32) for shape in shape...]
where the time goes in v7:
time: 32.1 us; the launch traced here: 31.9 us
  Pallas kernels  31.9 us (99%)
    pallas_call x1, Pallas kernels, on_device(): pl.pallas_call(body, out_shape=[pltpu.VMEM(shape, f32) for shape in shape...  30.3 us
    pallas_call x1, Pallas kernels, on_device(): pl.pallas_call(advection, out_shape=jax.ShapeDtypeStruct((C, LINES, Z), f...  1.68 us

profile of v7, /device:TPU:1, one launch (start us, length us, event | category | flops | bytes accessed | tf_op | source)
XLA Modules:
  0.0 31.9 jit_solution(4669062863431877414)
XLA Ops:
  0.0 30.3 %shard_map.55 = (f32[6592,128]{1,0:T(8,128)S(1)}, f32[512,128]{1,0:T(8,128)S(1)}, f32[544,128]{1,0:T(8,128)S(1)}, f32[544,128]{1,0:T(8,128)S(1)}, f32[776,128]{1...) custom-call(f32[6,512,128]{2,1,0:T(8,128)} %bitcast.6, ...), custom_call_target="tpu_custom_call" | custom-call | tf_op jit(solution)/shard_map/pallas_call | solution.py:614
  30.3 1.7 %shard_map.56 = f32[6,512,128]{2,1,0:T(8,128)} custom-call(f32[6592,128]{1,0:T(8,128)S(1)} %get-tuple-element.13.fb, f32[512,128]{1,0:T(8,128)S(1)} %get-tuple-element.14.c0, f32[544,128]{1,0:T(8,128)S(1)} %get-tuple-element.15.ax, f32[544,128]{1,0:T(8,128)S(1)} %get-tuple-element.16.bx, f32[776,128]{1,0:T(8,128)S(1)} %get-tuple-element.17.ayp, ...), custom_call_target="tpu_custom_call" | custom-call | tf_op jit(solution)/shard_map/pallas_call | solution.py:635

commit v8 on v7

--- a/solution.py
+++ b/solution.py
@@ -287,49 +287,6 @@
     for e in edges:
         e.start()
 
-    def x_factor():
-        rows = pl.ds(0, 32)
-        one = jnp.ones((32, Z), f32)
-
-        def up(x, carry):
-            theta, delta = carry
-            xb[x, rows, :] = theta
-            delta = delta + xe[x, rows, :] * theta
-            return theta + delta, delta
-
-        theta, _ = lax.fori_loop(0, X, up, (one, one), unroll=8)
-        rn = 1.0 / theta
-        xr[rows, :] = rn
-
-        def down(step, carry):
-            x = X - 1 - step
-            phi, delta, after, _ = carry
-            cell = xe[x, rows, :]
-            a = phi * rn
-            b = xb[x, rows, :] * rn
-            xa[x, rows, :] = a
-            xb[x, rows, :] = b
-            xw[x, rows, :] = 1.0 / (b * after)
-            xo[x, rows, :] = b * cell
-            delta = delta + cell * phi
-            return phi + delta, delta, b, a
-
-        _, _, _, first = lax.fori_loop(0, X, down, (one, one, one, one), unroll=8)
-        return first, rn
-
-    pairs[0].wait_recv()
-    for x in range(X):
-        xe[x, 0:Y, :] = ec[x * Y : (x + 1) * Y, :]
-        xe[x, 16:24, :] = jnp.broadcast_to(fre[1, x : x + 1, :], (8, Z))
-        xe[x, 24:32, :] = jnp.broadcast_to(fre[0, x : x + 1, :], (8, Z))
-    first, rn = x_factor()
-    for t, part in enumerate((first, rn, xb[X - 1])):
-        for r in range(2):
-            csx[pl.ds(4 * t + r, 8, stride=16), :] = part[r * 8 : r * 8 + 8]
-        csx[pl.ds(4 * t + 2, C, stride=16), :] = part[16 : 16 + C]
-        csx[pl.ds(C * 16 + 4 * t + 2, 8 - C, stride=16), :] = part[24 : 32 - C]
-        csx[pl.ds(4 * t + 3, 8, stride=16), :] = part[24:32]
-
     loads[2].wait()
     loads[3].wait()
     fsy[0] = upw[1, pl.ds(0, X, stride=Y), :].astype(f32) * cou[1, pl.ds(0, X, stride=Y), :]
@@ -337,7 +294,6 @@
     fsx[0] = upw[0, 0:Y, :].astype(f32) * cou[0, 0:Y, :] * ec[0:Y, :]
     fsx[1] = (1.0 - upw[0, LINES - Y : LINES, :].astype(f32)) * cou[0, LINES - Y : LINES, :] * ec[LINES - Y : LINES, :]
 
-    send_all(*coup_x)
     for f in faces:
         f.start()
 
@@ -377,18 +333,6 @@
             results[m * pitch + half : m * pitch + 2 * half, :] = later
             later = gl[1, m, 0:half, :] + factors[2, m, 0:half, :] * later
             results[m * pitch : m * pitch + half, :] = gl[0, m, 0:half, :] + factors[3, m, 0:half, :] * later
-
-    recv_all(*coup_y)
-    reduce_factor(NJ, 8, (C, C), HALF, rcy, ky)
-
-    recv_all(*tot_y)
-    reduce_solve(NJ, PACK, HALF, tty, ky, oty)
-    send_all(*ret_y)
-
-    recv_all(*coup_x)
-    reduce_factor(NI, 16, (C, C, 1, 1), HALF_X, rcx, kx)
-    pairs[1].wait_recv()
-    pairs[2].wait_recv()
 
     low_ok = jnp.where(j > 0, 1.0, 0.0).astype(f32)
     high_ok = jnp.where(j < NJ - 1, 1.0, 0.0).astype(f32)
@@ -411,10 +355,6 @@
         return 0
 
     lax.fori_loop(0, X, coefficients, 0, unroll=8)
-    bx[0:Y, :] = frx[1]
-    ax[(X + 1) * Y : (X + 2) * Y, :] = frx[0]
-    byp[pl.ds(7, X, stride=PAD), :] = fry[1] * low_ok
-    ayp[pl.ds(PAD, X, stride=PAD), :] = fry[0] * high_ok
     ayh[...] = jnp.zeros_like(ayh)
 
     for q in range(4):
@@ -430,6 +370,58 @@
             for c in range(C):
                 live[c] = live[c] + weight * yf[c, y, xs, :]
                 ay[c, cells, :] = live[c] * finish
+
+    recv_all(*coup_y)
+    reduce_factor(NJ, 8, (C, C), HALF, rcy, ky)
+
+    recv_all(*tot_y)
+    reduce_solve(NJ, PACK, HALF, tty, ky, oty)
+    send_all(*ret_y)
+
+    def x_factor():
+        rows = pl.ds(0, 32)
+        one = jnp.ones((32, Z), f32)
+
+        def up(x, carry):
+            theta, delta = carry
+            xb[x, rows, :] = theta
+            delta = delta + xe[x, rows, :] * theta
+            return theta + delta, delta
+
+        theta, _ = lax.fori_loop(0, X, up, (one, one), unroll=8)
+        rn = 1.0 / theta
+        xr[rows, :] = rn
+
+        def down(step, carry):
+            x = X - 1 - step
+            phi, delta, after, _ = carry
+            cell = xe[x, rows, :]
+            a = phi * rn
+            b = xb[x, rows, :] * rn
+            xa[x, rows, :] = a
+            xb[x, rows, :] = b
+            xw[x, rows, :] = 1.0 / (b * after)
+            xo[x, rows, :] = b * cell
+            delta = delta + cell * phi
+            return phi + delta, delta, b, a
+
+        _, _, _, first = lax.fori_loop(0, X, down, (one, one, one, one), unroll=8)
+        return first, rn
+
+    pairs[0].wait_recv()
+    for x in range(X):
+        xe[x, 0:Y, :] = ec[x * Y : (x + 1) * Y, :]
+        xe[x, 16:24, :] = jnp.broadcast_to(fre[1, x : x + 1, :], (8, Z))
+        xe[x, 24:32, :] = jnp.broadcast_to(fre[0, x : x + 1, :], (8, Z))
+    first, rn = x_factor()
+    for t, part in enumerate((first, rn, xb[X - 1])):
+        for r in range(2):
+            csx[pl.ds(4 * t + r, 8, stride=16), :] = part[r * 8 : r * 8 + 8]
+        csx[pl.ds(4 * t + 2, C, stride=16), :] = part[16 : 16 + C]
+        csx[pl.ds(C * 16 + 4 * t + 2, 8 - C, stride=16), :] = part[24 : 32 - C]
+        csx[pl.ds(4 * t + 3, 8, stride=16), :] = part[24:32]
+
+    send_all(*coup_x)
 
     def x_totals(x, carry):
         heads, tails = carry
@@ -511,6 +503,8 @@
         return tuple(out), halo
 
     lax.fori_loop(0, X, x_prefix, ((none,) * C, none), unroll=8)
+    recv_all(*coup_x)
+    reduce_factor(NI, 16, (C, C, 1, 1), HALF_X, rcx, kx)
     sent_all(*coup_y)
     sent_all(*coup_x)
     sent_all(*tot_y)
@@ -520,6 +514,12 @@
     recv_all(*tot_x)
     reduce_solve(NI, STEP_X, HALF_X, ttx, kx, otx)
     send_all(*ret_x)
+    pairs[1].wait_recv()
+    pairs[2].wait_recv()
+    bx[0:Y, :] = frx[1]
+    ax[(X + 1) * Y : (X + 2) * Y, :] = frx[0]
+    byp[pl.ds(7, X, stride=PAD), :] = fry[1] * low_ok
+    ayp[pl.ds(PAD, X, stride=PAD), :] = fry[0] * high_ok
 
     sent_all(*tot_x)
     recv_all(*ret_x)

time: 32.1 us -> 30.3 us (0.944)
  Pallas kernels: 31.9 us -> 30.2 us
    pallas_call x1, Pallas kernels: 30.3 us -> 28.5 us  [on_device(): pl.pallas_call(body, out_shape=[pltpu.VMEM(shape, f32) for shape in shape...]
where the time goes in v8:
time: 30.3 us; the launch traced here: 30.2 us
  Pallas kernels  30.2 us (100%)
    pallas_call x1, Pallas kernels, on_device(): pl.pallas_call(body, out_shape=[pltpu.VMEM(shape, f32) for shape in shape...  28.5 us
    pallas_call x1, Pallas kernels, on_device(): pl.pallas_call(advection, out_shape=jax.ShapeDtypeStruct((C, LINES, Z), f...  1.68 us

profile of v8, /device:TPU:1, one launch (start us, length us, event | category | flops | bytes accessed | tf_op | source)
XLA Modules:
  0.0 30.2 jit_solution(13291071503010515542)
XLA Ops:
  0.0 28.5 %shard_map.55 = (f32[6592,128]{1,0:T(8,128)S(1)}, f32[512,128]{1,0:T(8,128)S(1)}, f32[544,128]{1,0:T(8,128)S(1)}, f32[544,128]{1,0:T(8,128)S(1)}, f32[776,128]{1...) custom-call(f32[6,512,128]{2,1,0:T(8,128)} %bitcast.6, ...), custom_call_target="tpu_custom_call" | custom-call | tf_op jit(solution)/shard_map/pallas_call | solution.py:614
  28.5 1.7 %shard_map.56 = f32[6,512,128]{2,1,0:T(8,128)} custom-call(f32[6592,128]{1,0:T(8,128)S(1)} %get-tuple-element.13.fb, f32[512,128]{1,0:T(8,128)S(1)} %get-tuple-element.14.c0, f32[544,128]{1,0:T(8,128)S(1)} %get-tuple-element.15.ax, f32[544,128]{1,0:T(8,128)S(1)} %get-tuple-element.16.bx, f32[776,128]{1,0:T(8,128)S(1)} %get-tuple-element.17.ayp, ...), custom_call_target="tpu_custom_call" | custom-call | tf_op jit(solution)/shard_map/pallas_call | solution.py:635

commit v9 on v8

--- a/solution.py
+++ b/solution.py
@@ -33,13 +33,13 @@
 
 def body(
     cot_h, dif_h, pha_h, cou_h, upw_h,
-    fb, c0, ax, bx, ayp, byp, azn, bzp,
+    ay, ayh, xl, xo, lr, lrh, c0, ax, bx, ayp, byp, azn, bzp,
     cot, dif, pha, cou, upw, ec,
     et, zt, zw, zo, zb, tri,
-    yb, ya, yw, yo, yr, yf, ay, ayh, ynl, ynr, ends,
-    xe, xb, xa, xw, xo, xr,
+    yb, ya, yw, yo, yr, yf, ynl, ynr, ends,
+    xe, xb, xa, xw, xr,
     csy, csx, rcy, rcx, ky, kx, gl,
-    sty, tty, oty, rty, stx, ttx, otx, rtx, ext,
+    sty, tty, oty, rty, stx, ttx, otx, rtx,
     fse, fre, fsy, fry, fsx, frx,
     in_sem,
     sent, came,
@@ -521,47 +521,55 @@
     byp[pl.ds(7, X, stride=PAD), :] = fry[1] * low_ok
     ayp[pl.ds(PAD, X, stride=PAD), :] = fry[0] * high_ok
 
+    def x_local(step, carry):
+        x = X - 1 - step
+        live, halo, summed = carry
+        rows = pl.ds(pl.multiple_of(x * Y, Y), Y)
+        weight, finish = xw[x], xo[x]
+        summed = summed + weight
+        xl[x] = finish * (summed * xr[...])
+        out = []
+        for c in range(C):
+            value = live[c] + weight[0:Y] * ay[c, rows, :]
+            ay[c, rows, :] = value * finish[0:Y]
+            out.append(value)
+        halo = halo + weight[16:32] * ayh[rows, :]
+        ayh[rows, :] = halo * finish[16:32]
+        return tuple(out), halo, summed
+
+    lax.fori_loop(0, X, x_local, ((none,) * C, none, jnp.zeros((32, Z), f32)), unroll=4)
     sent_all(*tot_x)
     recv_all(*ret_x)
 
-    lefts, rights = [], []
+    for end in range(2):
+        for c in range(C):
+            for r in range(2):
+                lr[end, c, r * 8 : r * 8 + 8, :] = rtx[pl.ds(end * HALF_X + r * C + c, 8, stride=STEP_X), :]
+        at = end * HALF_X + HALF
+        lrh[end] = jnp.zeros((16, Z), f32)
+        lrh[end, 0:C, :] = rtx[pl.ds(at, C, stride=STEP_X), :]
+        lrh[end, 8 : 16 - C, :] = rtx[pl.ds(C * STEP_X + at, 8 - C, stride=STEP_X), :]
+        lrh[end, 16 - C : 8 + C, :] = rtx[pl.ds(at + 1, 2 * C - 8, stride=STEP_X), :]
+    sent_all(*ret_x)
+
+
+def advection(ay, ayh, xl, xo, lr, lrh, c0, ax, bx, ayp, byp, azn, bzp, out_h, fb, out, sem):
     for c in range(C):
-        left = jnp.concatenate([rtx[pl.ds(r * C + c, 8, stride=STEP_X), :] for r in range(2)], axis=0)
-        right = jnp.concatenate([rtx[pl.ds(HALF_X + r * C + c, 8, stride=STEP_X), :] for r in range(2)], axis=0)
-        fb[pl.ds(c * PITCH + 8, Y), :] = left
-        fb[pl.ds(c * PITCH + (X + 1) * PAD + 8, Y), :] = right
-        lefts.append(left * xr[0:Y, :])
-        rights.append(right)
-    for end in range(2):
-        at = end * HALF_X + HALF
-        ext[end, 0:C, :] = rtx[pl.ds(at, C, stride=STEP_X), :]
-        ext[end, 8 : 16 - C, :] = rtx[pl.ds(C * STEP_X + at, 8 - C, stride=STEP_X), :]
-        ext[end, 16 - C : 8 + C, :] = rtx[pl.ds(at + 1, 2 * C - 8, stride=STEP_X), :]
-    left_halo = ext[0] * xr[16:32, :]
-    right_halo = ext[1]
-
-    def x_finish(step, carry):
-        x = X - 1 - step
-        live, halo = carry
+        fb[pl.ds(c * PITCH + 8, Y), :] = lr[0, c]
+        fb[pl.ds(c * PITCH + (X + 1) * PAD + 8, Y), :] = lr[1, c]
+
+    def fill(x, _):
         rows = pl.ds(pl.multiple_of(x * Y, Y), Y)
-        weight, finish = xw[x, 0:Y, :], xo[x, 0:Y, :]
-        out = []
-        for c in range(C):
-            value = live[c] + weight * (ay[c, rows, :] + lefts[c])
-            fb[pl.ds(pl.multiple_of(c * PITCH + (x + 1) * PAD + 8, 8), Y), :] = value * finish
-            out.append(value)
-        halo = halo + xw[x, 16:32, :] * (ayh[rows, :] + left_halo)
-        edge = halo * xo[x, 16:32, :]
+        left, right = xl[x], xo[x]
+        for c in range(C):
+            fb[pl.ds(pl.multiple_of(c * PITCH + (x + 1) * PAD + 8, 8), Y), :] = (
+                ay[c, rows, :] + left[0:Y] * lr[0, c] + right[0:Y] * lr[1, c]
+            )
+        edge = ayh[rows, :] + left[16:32] * lrh[0] + right[16:32] * lrh[1]
         fb[pl.ds((x + 1) * PAD + 7, 8, stride=PITCH), :] = edge[0:8]
         fb[pl.ds((x + 2) * PAD, 8, stride=PITCH), :] = edge[8:16]
-        return tuple(out), halo
-
-    lax.fori_loop(0, X, x_finish, (tuple(rights), right_halo), unroll=4)
-
-    sent_all(*ret_x)
-
-
-def advection(fb, c0, ax, bx, ayp, byp, azn, bzp, out_h, out, sem):
+        return 0
+
     def advect(x, _):
         rows = pl.ds(pl.multiple_of(x * Y, Y), Y)
         middle = c0[rows, :]
@@ -583,6 +591,7 @@
 
     stores = []
     for part in range(4):
+        lax.fori_loop(part * 8 + min(part, 1), min(part * 8 + 9, X), fill, 0, unroll=True)
         lax.fori_loop(part * 8, part * 8 + 8, advect, 0, unroll=8)
         rows = pl.ds(part * 8 * Y, 8 * Y)
         store = pltpu.make_async_copy(out.at[:, rows, :], out_h.at[:, rows, :], sem.at[part])
@@ -601,16 +610,17 @@
         vm(C, LINES, Z), vm(LINES, Z), vm(LINES, Z, dtype=jnp.int32), vm(3, LINES, Z), vm(3, LINES, Z, dtype=jnp.int32),
         vm(LINES, Z),
         vm(LINES // Z, Z, Z), vm(LINES, Z), vm(LINES, Z), vm(LINES, Z), vm(C, LINES, Z), vm(2, 2 * Z, Z, dtype=jnp.bfloat16),
-        vm(Y, X, Z), vm(Y, X, Z), vm(Y, X, Z), vm(Y, X, Z), vm(X, Z), vm(C, Y, X, Z), vm(C, LINES, Z), vm(X * 16, Z), vm(LINES, Z), vm(LINES, Z), vm(4, LINES, Z),
-        vm(X, 32, Z), vm(X, 32, Z), vm(X, 32, Z), vm(X, 32, Z), vm(X, 32, Z), vm(32, Z),
+        vm(Y, X, Z), vm(Y, X, Z), vm(Y, X, Z), vm(Y, X, Z), vm(X, Z), vm(C, Y, X, Z), vm(LINES, Z), vm(LINES, Z), vm(4, LINES, Z),
+        vm(X, 32, Z), vm(X, 32, Z), vm(X, 32, Z), vm(X, 32, Z), vm(32, Z),
         vm(NJ * 8, Z), vm(NI * 16, Z), vm(NJ * 8, Z), vm(NI * 16, Z), vm(6, NJ, 16, Z), vm(6, NI, 16, Z), vm(2, NJ, 16, Z),
         vm(NJ * PACK, Z), vm(NJ * PACK, Z), vm(NJ * PACK, Z), vm(NJ * PACK, Z),
-        vm(NI * STEP_X, Z), vm(NI * STEP_X, Z), vm(NI * STEP_X, Z), vm(NI * STEP_X, Z), vm(2, 16, Z),
+        vm(NI * STEP_X, Z), vm(NI * STEP_X, Z), vm(NI * STEP_X, Z), vm(NI * STEP_X, Z),
         vm(2, X, Z), vm(2, X, Z), vm(2, X, Z), vm(2, X, Z), vm(2, Y, Z), vm(2, Y, Z),
         dma((8,)), dma((9,)), dma((9,)),
     ]
     vmem = pl.BlockSpec(memory_space=pltpu.VMEM)
-    shapes = [(8 * PITCH, Z), (LINES, Z), (LINES + 2 * Y, Z), (LINES + 2 * Y, Z), (X * PAD + 8, Z), (X * PAD + 8, Z), (LINES, Z), (LINES, Z)]
+    shapes = [(C, LINES, Z), (X * 16, Z), (X, 32, Z), (X, 32, Z), (2, C, Y, Z), (2, 16, Z)]
+    shapes += [(LINES, Z), (LINES + 2 * Y, Z), (LINES + 2 * Y, Z), (X * PAD + 8, Z), (X * PAD + 8, Z), (LINES, Z), (LINES, Z)]
     parts = pl.pallas_call(
         body,
         out_shape=[pltpu.VMEM(shape, f32) for shape in shapes],
@@ -637,8 +647,8 @@
         out_shape=jax.ShapeDtypeStruct((C, LINES, Z), f32),
         in_specs=[vmem] * len(shapes),
         out_specs=pl.BlockSpec(memory_space=pl.ANY),
-        scratch_shapes=[vm(C, LINES, Z), dma((4,))],
-        compiler_params=pltpu.CompilerParams(vmem_limit_bytes=8 * 1024 * 1024),
+        scratch_shapes=[vm(8 * PITCH, Z), vm(C, LINES, Z), dma((4,))],
+        compiler_params=pltpu.CompilerParams(vmem_limit_bytes=12 * 1024 * 1024),
     )(*(pltpu.with_memory_space_constraint(part, pltpu.VMEM) for part in parts))
     return out.reshape(C, X, Y, Z)
 

time: 30.3 us -> 30.2 us (level)
    pallas_call x1, Pallas kernels: 28.5 us -> 28.1 us  [on_device(): pl.pallas_call(body, out_shape=[pltpu.VMEM(shape, f32) for shape in shape...]
where the time goes in v9:
time: 30.2 us; the launch traced here: 30.1 us
  Pallas kernels  30.1 us (100%)
    pallas_call x1, Pallas kernels, on_device(): pl.pallas_call(body, out_shape=[pltpu.VMEM(shape, f32) for shape in shape...  28.1 us
    pallas_call x1, Pallas kernels, on_device(): pl.pallas_call(advection, out_shape=jax.ShapeDtypeStruct((C, LINES, Z), f...  1.93 us

profile of v9, /device:TPU:1, one launch (start us, length us, event | category | flops | bytes accessed | tf_op | source)
XLA Modules:
  0.0 30.1 jit_solution(1528085349895723348)
XLA Ops:
  0.0 28.1 %shard_map.55 = (f32[6,512,128]{2,1,0:T(8,128)S(1)}, f32[512,128]{1,0:T(8,128)S(1)}, f32[32,32,128]{2,1,0:T(8,128)S(1)}, f32[32,32,128]{2,1,0:T(8,128)S(1)}, f32...) custom-call(f32[6,512,128]{2,1,0:T(8,128)} %bitcast.6, ...), custom_call_target="tpu_custom_call" | custom-call | tf_op jit(solution)/shard_map/pallas_call | solution.py:624
  28.2 1.9 %shard_map.56 = f32[6,512,128]{2,1,0:T(8,128)} custom-call(f32[6,512,128]{2,1,0:T(8,128)S(1)} %get-tuple-element.18.ay, f32[512,128]{1,0:T(8,128)S(1)} %get-tuple-element.19.ayh, f32[32,32,128]{2,1,0:T(8,128)S(1)} %get-tuple-element.20.xl, f32[32,32,128]{2,1,0:T(8,128)S(1)} %get-tuple-element.21.xo, f32[2,6,16,128]{3,2,1,0:T(8,128)S(1)} %get-tuple-element.22.lr, ...), custom_call_target="tpu_custom_call" | custom-call | tf_op jit(solution)/shard_map/pallas_call | solution.py:645

commit v10 on v8

--- a/solution.py
+++ b/solution.py
@@ -21,7 +21,6 @@
 STEP_X = 32
 f32 = jnp.float32
 FAR = sorted(((a, b) for a in range(4) for b in range(4) if a or b), key=lambda d: -min(d[0], 4 - d[0]) - min(d[1], 4 - d[1]))
-ORDER = (0, 2, 1, 3)
 FAR_X = [(2, 1), (2, 0), (3, 1), (1, 1), (3, 0), (1, 0), (0, 1)]
 
 
@@ -56,27 +55,19 @@
         pltpu.make_async_copy(upw_h, upw, in_sem.at[3]),
     ]
     quarters = [pl.ds(q * 8 * Y, 8 * Y) for q in range(4)]
-    fields = [
-        pltpu.make_async_copy(cot_h.at[:, rows, :], cot.at[:, rows, :], in_sem.at[4 + q])
-        for q, rows in enumerate(quarters)
-    ]
+    field = pltpu.make_async_copy(cot_h, cot, in_sem.at[4])
     loads[0].start()
     loads[1].start()
-    for q in ORDER:
-        fields[q].start()
+    field.start()
 
     barrier = pltpu.get_barrier_semaphore()
 
-    def greet_y(d, _):
-        pl.semaphore_signal(barrier, inc=1, device_id=(i, lax.rem(j + d, NJ)), device_id_type=MESH)
-        return 0
-
-    def greet_x(d, _):
-        pl.semaphore_signal(barrier, inc=1, device_id=(lax.rem(i + d, NI), j), device_id_type=MESH)
-        return 0
-
-    lax.fori_loop(1, NJ, greet_y, 0)
-    lax.fori_loop(1, NI, greet_x, 0)
+    for a, b in FAR:
+        to = lax.rem(j // 4 + a, 4) * 4 + lax.rem(j + b, 4)
+        pl.semaphore_signal(barrier, inc=1, device_id={"gy": to}, device_id_type=MESH)
+    for a, b in FAR_X:
+        to = lax.rem(i // 2 + a, 4) * 2 + lax.rem(i + b, 2)
+        pl.semaphore_signal(barrier, inc=1, device_id={"gx": to}, device_id_type=MESH)
 
     loads[0].wait()
     loads[1].wait()
@@ -268,8 +259,7 @@
             sty[pl.ds(at + c, 8, stride=PACK), :] = heads[c]
             sty[pl.ds(at + HALF + c, 8, stride=PACK), :] = tails[c]
 
-    for q in ORDER:
-        fields[q].wait()
+    field.wait()
     loads[2].start()
     loads[3].start()
     z_lower(0)
@@ -607,7 +597,7 @@
         vm(NJ * PACK, Z), vm(NJ * PACK, Z), vm(NJ * PACK, Z), vm(NJ * PACK, Z),
         vm(NI * STEP_X, Z), vm(NI * STEP_X, Z), vm(NI * STEP_X, Z), vm(NI * STEP_X, Z), vm(2, 16, Z),
         vm(2, X, Z), vm(2, X, Z), vm(2, X, Z), vm(2, X, Z), vm(2, Y, Z), vm(2, Y, Z),
-        dma((8,)), dma((9,)), dma((9,)),
+        dma((5,)), dma((9,)), dma((9,)),
     ]
     vmem = pl.BlockSpec(memory_space=pltpu.VMEM)
     shapes = [(8 * PITCH, Z), (LINES, Z), (LINES + 2 * Y, Z), (LINES + 2 * Y, Z), (X * PAD + 8, Z), (X * PAD + 8, Z), (LINES, Z), (LINES, Z)]

time: 30.3 us -> 30.3 us (level)
  no operation moved by 1% of the time
where the time goes in v10:
time: 30.3 us; the launch traced here: 30.2 us
  Pallas kernels  30.2 us (100%)
    pallas_call x1, Pallas kernels, on_device(): pl.pallas_call(body, out_shape=[pltpu.VMEM(shape, f32) for shape in shape...  28.5 us
    pallas_call x1, Pallas kernels, on_device(): pl.pallas_call(advection, out_shape=jax.ShapeDtypeStruct((C, LINES, Z), f...  1.68 us

profile of v10, /device:TPU:1, one launch (start us, length us, event | category | flops | bytes accessed | tf_op | source)
XLA Modules:
  0.0 30.2 jit_solution(2088578849187933776)
XLA Ops:
  0.0 28.5 %shard_map.55 = (f32[6592,128]{1,0:T(8,128)S(1)}, f32[512,128]{1,0:T(8,128)S(1)}, f32[544,128]{1,0:T(8,128)S(1)}, f32[544,128]{1,0:T(8,128)S(1)}, f32[776,128]{1...) custom-call(f32[6,512,128]{2,1,0:T(8,128)} %bitcast.6, ...), custom_call_target="tpu_custom_call" | custom-call | tf_op jit(solution)/shard_map/pallas_call | solution.py:604
  28.5 1.7 %shard_map.56 = f32[6,512,128]{2,1,0:T(8,128)} custom-call(f32[6592,128]{1,0:T(8,128)S(1)} %get-tuple-element.13.fb, f32[512,128]{1,0:T(8,128)S(1)} %get-tuple-element.14.c0, f32[544,128]{1,0:T(8,128)S(1)} %get-tuple-element.15.ax, f32[544,128]{1,0:T(8,128)S(1)} %get-tuple-element.16.bx, f32[776,128]{1,0:T(8,128)S(1)} %get-tuple-element.17.ayp, ...), custom_call_target="tpu_custom_call" | custom-call | tf_op jit(solution)/shard_map/pallas_call | solution.py:625

commit v11 on v8

--- a/solution.py
+++ b/solution.py
@@ -280,8 +280,8 @@
         y_totals(q)
 
     pl.semaphore_wait(barrier, NI + NJ - 2)
+    send_all(*coup_y)
     send_all(*tot_y)
-    send_all(*coup_y)
     fse[0] = ec[pl.ds(0, X, stride=Y), :]
     fse[1] = ec[pl.ds(Y - 1, X, stride=Y), :]
     for e in edges:

time: 30.3 us -> 30.1 us (level)
  no operation moved by 1% of the time
where the time goes in v11:
time: 30.1 us; the launch traced here: 30 us
  Pallas kernels  30 us (100%)
    pallas_call x1, Pallas kernels, on_device(): pl.pallas_call(body, out_shape=[pltpu.VMEM(shape, f32) for shape in shape...  28.3 us
    pallas_call x1, Pallas kernels, on_device(): pl.pallas_call(advection, out_shape=jax.ShapeDtypeStruct((C, LINES, Z), f...  1.68 us

profile of v11, /device:TPU:1, one launch (start us, length us, event | category | flops | bytes accessed | tf_op | source)
XLA Modules:
  0.0 30.0 jit_solution(710299388803391872)
XLA Ops:
  0.0 28.3 %shard_map.55 = (f32[6592,128]{1,0:T(8,128)S(1)}, f32[512,128]{1,0:T(8,128)S(1)}, f32[544,128]{1,0:T(8,128)S(1)}, f32[544,128]{1,0:T(8,128)S(1)}, f32[776,128]{1...) custom-call(f32[6,512,128]{2,1,0:T(8,128)} %bitcast.6, ...), custom_call_target="tpu_custom_call" | custom-call | tf_op jit(solution)/shard_map/pallas_call | solution.py:614
  28.3 1.7 %shard_map.56 = f32[6,512,128]{2,1,0:T(8,128)} custom-call(f32[6592,128]{1,0:T(8,128)S(1)} %get-tuple-element.13.fb, f32[512,128]{1,0:T(8,128)S(1)} %get-tuple-element.14.c0, f32[544,128]{1,0:T(8,128)S(1)} %get-tuple-element.15.ax, f32[544,128]{1,0:T(8,128)S(1)} %get-tuple-element.16.bx, f32[776,128]{1,0:T(8,128)S(1)} %get-tuple-element.17.ayp, ...), custom_call_target="tpu_custom_call" | custom-call | tf_op jit(solution)/shard_map/pallas_call | solution.py:635

commit v12 on v8

--- a/solution.py
+++ b/solution.py
@@ -474,7 +474,7 @@
         )
 
     heads, tails, *edge_pair = lax.fori_loop(
-        0, X, end_totals, (tuple(heads), tuple(tails), none, none), unroll=8
+        0, X, end_totals, (tuple(heads), tuple(tails), none, none), unroll=32
     )
     for c in range(C):
         for r in range(2):
@@ -556,7 +556,7 @@
         fb[pl.ds((x + 2) * PAD, 8, stride=PITCH), :] = edge[8:16]
         return tuple(out), halo
 
-    lax.fori_loop(0, X, x_finish, (tuple(rights), right_halo), unroll=4)
+    lax.fori_loop(0, X, x_finish, (tuple(rights), right_halo), unroll=8)
 
     sent_all(*ret_x)
 

time: 30.3 us -> 30.3 us (level)
  no operation moved by 1% of the time
where the time goes in v12:
time: 30.3 us; the launch traced here: 30.2 us
  Pallas kernels  30.2 us (100%)
    pallas_call x1, Pallas kernels, on_device(): pl.pallas_call(body, out_shape=[pltpu.VMEM(shape, f32) for shape in shape...  28.5 us
    pallas_call x1, Pallas kernels, on_device(): pl.pallas_call(advection, out_shape=jax.ShapeDtypeStruct((C, LINES, Z), f...  1.68 us

profile of v12, /device:TPU:1, one launch (start us, length us, event | category | flops | bytes accessed | tf_op | source)
XLA Modules:
  0.0 30.2 jit_solution(12786495373566794473)
XLA Ops:
  0.0 28.5 %shard_map.55 = (f32[6592,128]{1,0:T(8,128)S(1)}, f32[512,128]{1,0:T(8,128)S(1)}, f32[544,128]{1,0:T(8,128)S(1)}, f32[544,128]{1,0:T(8,128)S(1)}, f32[776,128]{1...) custom-call(f32[6,512,128]{2,1,0:T(8,128)} %bitcast.6, ...), custom_call_target="tpu_custom_call" | custom-call | tf_op jit(solution)/shard_map/pallas_call | solution.py:614
  28.5 1.7 %shard_map.56 = f32[6,512,128]{2,1,0:T(8,128)} custom-call(f32[6592,128]{1,0:T(8,128)S(1)} %get-tuple-element.13.fb, f32[512,128]{1,0:T(8,128)S(1)} %get-tuple-element.14.c0, f32[544,128]{1,0:T(8,128)S(1)} %get-tuple-element.15.ax, f32[544,128]{1,0:T(8,128)S(1)} %get-tuple-element.16.bx, f32[776,128]{1,0:T(8,128)S(1)} %get-tuple-element.17.ayp, ...), custom_call_target="tpu_custom_call" | custom-call | tf_op jit(solution)/shard_map/pallas_call | solution.py:635
